TPU v7x, 32 devices: a whole 2x2x4 slice. The times are simulated.
32 devices in a mesh: seq: 16 (over z, y, core), fsdp: 2 (over x).
Axes of the slice: x: 2, y: 2, z: 4, core: 2. Of those that a mesh axis runs over, the one named last changes fastest.
Arguments:
- tokens: bfloat16 [4096, 1536], P(('seq', 'fsdp')), may hold values from -6 to 6
- cotangent: bfloat16 [4096, 1536], P(('seq', 'fsdp')), may hold values from -6 to 6
- lengths: int32 [2, 5], replicated, may hold values from 1 to 1920, as said below
- mix_weight: float32 [1, 1536, 3072], P(None, ('seq', 'fsdp')), may hold values from -0.078125 to 0.078125
- out_weight: float32 [1, 1536, 1536], P(None, ('seq', 'fsdp')), may hold values from -0.875 to 0.875
- in_weight: float32 [1, 1536, 8192], P(None, ('seq', 'fsdp')), may hold values from -0.078125 to 0.078125
- down_weight: float32 [1, 4096, 1536], P(None, ('seq', 'fsdp')), may hold values from -0.09375 to 0.09375
- norm_gains: float32 [1, 2, 1536], P(None, None, ('seq', 'fsdp')), may hold values from 0.5 to 6
- mix_first: float32 [1, 1536, 3072], P(None, ('seq', 'fsdp')), may hold values from -0.00012207031 to 0.00012207031
- out_first: float32 [1, 1536, 1536], P(None, ('seq', 'fsdp')), may hold values from -1.9073486e-05 to 1.9073486e-05
- in_first: float32 [1, 1536, 8192], P(None, ('seq', 'fsdp')), may hold values from -9.1552734e-05 to 9.1552734e-05
- down_first: float32 [1, 4096, 1536], P(None, ('seq', 'fsdp')), may hold values from -9.1552734e-05 to 9.1552734e-05
- norm_first: float32 [1, 2, 1536], P(None, None, ('seq', 'fsdp')), may hold values from -7.6293945e-05 to 7.6293945e-05
- mix_second: float32 [1, 1536, 3072], P(None, ('seq', 'fsdp')), may hold values from 3.8913012e-10 to 1.5565205e-09
- out_second: float32 [1, 1536, 1536], P(None, ('seq', 'fsdp')), may hold values from 4.8912163e-12 to 1.9564865e-11
- in_second: float32 [1, 1536, 8192], P(None, ('seq', 'fsdp')), may hold values from 9.6319334e-11 to 3.8527734e-10
- down_second: float32 [1, 4096, 1536], P(None, ('seq', 'fsdp')), may hold values from 9.6319334e-11 to 3.8527734e-10
- norm_second: float32 [1, 2, 1536], P(None, None, ('seq', 'fsdp')), may hold values from 7.705547e-11 to 3.082219e-10
Outputs:
- hidden_out: bfloat16 [4096, 1536], P(('seq', 'fsdp'))
- grad_tokens: float32 [4096, 1536], P(('seq', 'fsdp'))
- grad_norm: float32 [], replicated
- mix_grad: float32 [1, 1536, 3072], P(None, ('seq', 'fsdp'))
- mix_new: float32 [1, 1536, 3072], P(None, ('seq', 'fsdp'))
- mix_moment: float32 [1, 1536, 3072], P(None, ('seq', 'fsdp'))
- mix_square: float32 [1, 1536, 3072], P(None, ('seq', 'fsdp'))
- mix_copy: bfloat16 [1, 1536, 3072], P(None, ('seq', 'fsdp'))
- out_grad: float32 [1, 1536, 1536], P(None, ('seq', 'fsdp'))
- out_new: float32 [1, 1536, 1536], P(None, ('seq', 'fsdp'))
- out_moment: float32 [1, 1536, 1536], P(None, ('seq', 'fsdp'))
- out_square: float32 [1, 1536, 1536], P(None, ('seq', 'fsdp'))
- out_copy: bfloat16 [1, 1536, 1536], P(None, ('seq', 'fsdp'))
- in_grad: float32 [1, 1536, 8192], P(None, ('seq', 'fsdp'))
- in_new: float32 [1, 1536, 8192], P(None, ('seq', 'fsdp'))
- in_moment: float32 [1, 1536, 8192], P(None, ('seq', 'fsdp'))
- in_square: float32 [1, 1536, 8192], P(None, ('seq', 'fsdp'))
- in_copy: bfloat16 [1, 1536, 8192], P(None, ('seq', 'fsdp'))
- down_grad: float32 [1, 4096, 1536], P(None, ('seq', 'fsdp'))
- down_new: float32 [1, 4096, 1536], P(None, ('seq', 'fsdp'))
- down_moment: float32 [1, 4096, 1536], P(None, ('seq', 'fsdp'))
- down_square: float32 [1, 4096, 1536], P(None, ('seq', 'fsdp'))
- down_copy: bfloat16 [1, 4096, 1536], P(None, ('seq', 'fsdp'))
- norm_grad: float32 [1, 2, 1536], P(None, None, ('seq', 'fsdp'))
- norm_new: float32 [1, 2, 1536], P(None, None, ('seq', 'fsdp'))
- norm_moment: float32 [1, 2, 1536], P(None, None, ('seq', 'fsdp'))
- norm_square: float32 [1, 2, 1536], P(None, None, ('seq', 'fsdp'))
- norm_copy: bfloat16 [1, 2, 1536], P(None, None, ('seq', 'fsdp'))
Inputs may be any that keep to these rules, and one draw needn't show every extreme that they name: `lengths`: in each group one document, which one drawn from the seed, is 128 * (15) tokens long and begins within the group's first 64 tokens; every other document is at most 21 tokens long; the group's tokens after its documents are padding.
All inputs are finite; a program needn't handle non-finite values.
Results may differ from a plain program's by a relative error of at most 0.025.
The roundings to bfloat16 on the way count: a program that leaves them out, or rounds other values in their place, can miss the bound.
Values may be sent and summed in bfloat16 or wider, within the bound.
A program may use at most 448 MiB of HBM per device.

v0:
```python
import jax
import jax.numpy as jnp
from jax import lax
from jax.sharding import PartitionSpec as P

D = 1536
HEADS = 16
KV_HEADS = 8
HEAD_DIM = 96
FF = 4096
LAYERS = 1
STEP_NUMBER = 10


EPS_NORM = 1e-05
ROPE_BASE = 100000.0
FLOOR_SCORE = -1e30
LEARN_RATE = 0.05
OUT_RATE = 0.2
GAIN_RATE = 2.0
BETA_ONE = 0.9
BETA_TWO = 0.99
EPS_ADAM = 1e-08
WEIGHT_DECAY = 0.1
CLIP_NORM = 1.0


def doc_layout(places, doc_lens):
    doc_ends = jnp.cumsum(doc_lens)
    passed = (places[:, None] >= doc_ends[None, :]).astype(jnp.int32)
    segment = jnp.sum(passed, axis=1)
    offset = jnp.sum(passed * doc_lens[None, :], axis=1)
    return (segment, places - offset)


def rotate(vectors, places, direction):
    half_dim = vectors.shape[-1] // 2
    inverse = ROPE_BASE ** (-jnp.arange(half_dim, dtype=jnp.float32) * 2.0 / vectors.shape[-1])
    angles = places.astype(jnp.float32)[:, None] * inverse[None, :]
    cosine = jnp.cos(angles)[:, None, :]
    sine_term = direction * jnp.sin(angles)[:, None, :]
    former = vectors[..., :half_dim]
    latter = vectors[..., half_dim:]
    return jnp.concatenate(
        [former * cosine - latter * sine_term, latter * cosine + former * sine_term], axis=-1
    )


def normalize(values, gain):
    scale_rows = lax.rsqrt(jnp.mean(values * values, axis=-1, keepdims=True) + EPS_NORM)
    unit_rows = values * scale_rows
    return (unit_rows * gain, unit_rows, scale_rows)


def norm_backward(grad_normed, unit_rows, scale_rows, gain):
    grad_gain = jnp.sum(grad_normed * unit_rows, axis=0)
    grad_unit = grad_normed * gain
    grad_values = scale_rows * (
        grad_unit - unit_rows * jnp.mean(grad_unit * unit_rows, axis=-1, keepdims=True)
    )
    return (grad_gain, grad_values)


def masked_scores(queries, key_block, first_key, query_places, query_segment, doc_lens):
    block_rows = key_block.shape[0]
    key_places = first_key + jnp.arange(block_rows, dtype=jnp.int32)
    key_segment, unused_places = doc_layout(key_places, doc_lens)
    allowed = (query_segment[:, None] == key_segment[None, :]) & (
        key_places[None, :] <= query_places[:, None]
    )
    key_heads = key_block.reshape(block_rows, KV_HEADS, HEAD_DIM)
    raw_scores = jnp.einsum(
        "qkgd,skd->qkgs", queries, key_heads, preferred_element_type=jnp.float32
    ) * HEAD_DIM ** (-0.5)
    return (jnp.where(allowed[:, None, None, :], raw_scores, FLOOR_SCORE), allowed)


def fold_block(carry, key_block, value_block, first_key, setting):
    queries, query_places, query_segment, doc_lens = setting
    running, totals, accumulated = carry
    block_rows = key_block.shape[0]
    scores, allowed = masked_scores(
        queries, key_block, first_key, query_places, query_segment, doc_lens
    )
    newest = jnp.maximum(running, jnp.max(scores, axis=-1))
    factor = jnp.exp(running - newest)
    weights = jnp.where(allowed[:, None, None, :], jnp.exp(scores - newest[..., None]), 0.0)
    totals = totals * factor + jnp.sum(weights, axis=-1)
    value_heads = value_block.reshape(block_rows, KV_HEADS, HEAD_DIM)
    accumulated = accumulated * factor[..., None] + jnp.einsum(
        "qkgs,skd->qkgd",
        weights.astype(jnp.bfloat16),
        value_heads,
        preferred_element_type=jnp.float32,
    )
    return (newest, totals, accumulated)


def fold_piece(carry, key_rows, value_rows, start, setting):
    total_rows = key_rows.shape[0]
    block_rows = 512

    def step(inner_state, number):
        first_key = start + number * block_rows
        key_block = lax.dynamic_slice_in_dim(key_rows, number * block_rows, block_rows, 0)
        value_block = lax.dynamic_slice_in_dim(value_rows, number * block_rows, block_rows, 0)
        state_out = fold_block(inner_state, key_block, value_block, first_key, setting)
        return (state_out, None)

    carry, unused_out = lax.scan(step, carry, jnp.arange(total_rows // block_rows, dtype=jnp.int32))
    return carry


def fetch_layer(mix_weight, out_weight, norm_gains, in_weight, down_weight, layer_index):
    mix_full, out_full, gain_full, in_full, down_full = (
        lax.all_gather(
            mix_weight[layer_index].astype(jnp.bfloat16), ("seq", "fsdp"), axis=0, tiled=True
        ),
        lax.all_gather(
            out_weight[layer_index].astype(jnp.bfloat16), ("seq", "fsdp"), axis=0, tiled=True
        ),
        lax.all_gather(
            norm_gains[layer_index].astype(jnp.bfloat16), ("seq", "fsdp"), axis=1, tiled=True
        ),
        lax.all_gather(
            in_weight[layer_index].astype(jnp.bfloat16), ("seq", "fsdp"), axis=0, tiled=True
        ),
        lax.all_gather(
            down_weight[layer_index].astype(jnp.bfloat16), ("seq", "fsdp"), axis=0, tiled=True
        ),
    )
    return ((mix_full, out_full, gain_full), (in_full, down_full))


def layer_forward(stream, attn_set, mlp_set, context):
    query_places, query_segment, positions, keep_rows, doc_lens = context
    mix_full, out_full, gain_full = attn_set
    in_full, down_full = mlp_set
    row_count = stream.shape[0]
    key_width = KV_HEADS * HEAD_DIM
    groups_per = HEADS // KV_HEADS
    gain_attn = gain_full[0].astype(jnp.float32)
    gain_mlp = gain_full[1].astype(jnp.float32)
    normed, unit_attn, scale_attn = normalize(stream, gain_attn)
    normed_low = normed.astype(jnp.bfloat16)
    projected = jnp.dot(normed_low, mix_full, preferred_element_type=jnp.float32)
    queries = (
        rotate(projected[:, :D].reshape(row_count, HEADS, HEAD_DIM), positions, 1.0)
        .astype(jnp.bfloat16)
        .reshape(row_count, KV_HEADS, groups_per, HEAD_DIM)
    )
    keys_low = (
        rotate(
            projected[:, D : D + key_width].reshape(row_count, KV_HEADS, HEAD_DIM), positions, 1.0
        )
        .astype(jnp.bfloat16)
        .reshape(row_count, key_width)
    )
    values_low = projected[:, D + key_width :].astype(jnp.bfloat16)
    setting = (queries, query_places, query_segment, doc_lens)
    key_all, value_all = (
        lax.all_gather(keys_low, "seq", axis=0, tiled=True),
        lax.all_gather(values_low, "seq", axis=0, tiled=True),
    )
    start_carry = (
        jnp.full((row_count, KV_HEADS, groups_per), FLOOR_SCORE, jnp.float32),
        jnp.zeros((row_count, KV_HEADS, groups_per), jnp.float32),
        jnp.zeros((row_count, KV_HEADS, groups_per, HEAD_DIM), jnp.float32),
    )
    running, totals, accumulated = fold_piece(start_carry, key_all, value_all, 0, setting)
    log_total = running + jnp.log(totals)
    attended = (accumulated / totals[..., None]).reshape(row_count, D) * keep_rows
    attended_low = attended.astype(jnp.bfloat16)
    middle = stream + jnp.dot(attended_low, out_full, preferred_element_type=jnp.float32)
    normed_two, unit_mlp, scale_mlp = normalize(middle, gain_mlp)
    normed_two_low = normed_two.astype(jnp.bfloat16)
    gate_up = jnp.dot(normed_two_low, in_full, preferred_element_type=jnp.float32)
    hidden_low = (jax.nn.silu(gate_up[:, :FF]) * gate_up[:, FF:]).astype(jnp.bfloat16)
    result = middle + jnp.dot(hidden_low, down_full, preferred_element_type=jnp.float32)
    kv_saved = (key_all, value_all)
    saved = (
        normed_low,
        unit_attn,
        scale_attn,
        queries,
        keys_low,
        values_low,
        log_total,
        attended,
        attended_low,
        unit_mlp,
        scale_mlp,
        normed_two_low,
        gate_up,
        hidden_low,
        kv_saved,
    )
    return (result, saved)


def layer_backward(grad_stream, saved, attn_set, mlp_set, context):
    query_places, query_segment, positions, keep_rows, doc_lens = context
    mix_full, out_full, gain_full = attn_set
    in_full, down_full = mlp_set
    (
        normed_low,
        unit_attn,
        scale_attn,
        queries,
        keys_low,
        values_low,
        log_total,
        attended,
        attended_low,
        unit_mlp,
        scale_mlp,
        normed_two_low,
        gate_up,
        hidden_low,
        kv_saved,
    ) = saved
    row_count = grad_stream.shape[0]
    key_width = KV_HEADS * HEAD_DIM
    groups_per = HEADS // KV_HEADS
    score_scale = HEAD_DIM ** (-0.5)
    gain_attn = gain_full[0].astype(jnp.float32)
    gain_mlp = gain_full[1].astype(jnp.float32)
    grad_branch = grad_stream.astype(jnp.bfloat16)
    grad_down = jnp.einsum("nf,nd->fd", hidden_low, grad_branch, preferred_element_type=jnp.float32)
    grad_hidden = jnp.einsum(
        "nd,fd->nf", grad_branch, down_full, preferred_element_type=jnp.float32
    )
    gate_part = gate_up[:, :FF]
    up_part = gate_up[:, FF:]
    sigmoid_gate = jax.nn.sigmoid(gate_part)
    grad_gate = grad_hidden * up_part * sigmoid_gate * (1.0 + gate_part * (1.0 - sigmoid_gate))
    grad_up = grad_hidden * gate_part * sigmoid_gate
    grad_gate_up = jnp.concatenate([grad_gate, grad_up], axis=1).astype(jnp.bfloat16)
    grad_in = jnp.einsum(
        "nd,nf->df", normed_two_low, grad_gate_up, preferred_element_type=jnp.float32
    )
    grad_normed_two = jnp.einsum(
        "nf,df->nd", grad_gate_up, in_full, preferred_element_type=jnp.float32
    )
    mlp_part = (
        lax.psum_scatter(grad_in, ("seq", "fsdp"), scatter_dimension=0, tiled=True),
        lax.psum_scatter(grad_down, ("seq", "fsdp"), scatter_dimension=0, tiled=True),
    )
    grad_gain_mlp, grad_middle_norm = norm_backward(grad_normed_two, unit_mlp, scale_mlp, gain_mlp)
    grad_middle = grad_stream + grad_middle_norm
    attn_branch = grad_middle.astype(jnp.bfloat16)
    grad_out = jnp.einsum(
        "nd,ne->de", attended_low, attn_branch, preferred_element_type=jnp.float32
    )
    grad_attended = (
        jnp.einsum("ne,de->nd", attn_branch, out_full, preferred_element_type=jnp.float32)
        * keep_rows
    )
    grad_heads = grad_attended.astype(jnp.bfloat16).reshape(
        row_count, KV_HEADS, groups_per, HEAD_DIM
    )
    row_delta = jnp.sum(
        grad_heads.astype(jnp.float32)
        * attended.reshape(row_count, KV_HEADS, groups_per, HEAD_DIM),
        axis=-1,
    )
    key_all, value_all = kv_saved
    total_keys = key_all.shape[0]
    block_rows = 512

    def back_step(grad_queries, number):
        first_key = number * block_rows
        key_block = lax.dynamic_slice_in_dim(key_all, first_key, block_rows, 0)
        value_block = lax.dynamic_slice_in_dim(value_all, first_key, block_rows, 0)
        scores, allowed = masked_scores(
            queries, key_block, first_key, query_places, query_segment, doc_lens
        )
        soft_weight = jnp.where(
            allowed[:, None, None, :], jnp.exp(scores - log_total[..., None]), 0.0
        )
        value_heads = value_block.reshape(block_rows, KV_HEADS, HEAD_DIM)
        key_heads = key_block.reshape(block_rows, KV_HEADS, HEAD_DIM)
        grad_weight = jnp.einsum(
            "qkgd,skd->qkgs", grad_heads, value_heads, preferred_element_type=jnp.float32
        )
        grad_score = (soft_weight * (grad_weight - row_delta[..., None])).astype(jnp.bfloat16)
        state_out = grad_queries + jnp.einsum(
            "qkgs,skd->qkgd", grad_score, key_heads, preferred_element_type=jnp.float32
        )
        grad_key = (
            jnp.einsum("qkgs,qkgd->skd", grad_score, queries, preferred_element_type=jnp.float32)
            * score_scale
        )
        grad_value = jnp.einsum(
            "qkgs,qkgd->skd",
            soft_weight.astype(jnp.bfloat16),
            grad_heads,
            preferred_element_type=jnp.float32,
        )
        return (
            state_out,
            jnp.concatenate(
                [
                    grad_key.reshape(block_rows, key_width),
                    grad_value.reshape(block_rows, key_width),
                ],
                axis=1,
            ),
        )

    start_grad = jnp.zeros((row_count, KV_HEADS, groups_per, HEAD_DIM), jnp.float32)
    grad_queries, pair_blocks = lax.scan(
        back_step, start_grad, jnp.arange(total_keys // block_rows, dtype=jnp.int32)
    )
    pair_terms = pair_blocks.reshape(total_keys, 2 * key_width)
    pair_sums = lax.psum_scatter(pair_terms, "seq", scatter_dimension=0, tiled=True)
    grad_rot_queries = rotate(
        (grad_queries * score_scale).reshape(row_count, HEADS, HEAD_DIM), positions, -1.0
    ).reshape(row_count, D)
    grad_rot_keys = rotate(
        pair_sums[:, :key_width].reshape(row_count, KV_HEADS, HEAD_DIM), positions, -1.0
    ).reshape(row_count, key_width)
    grad_projected = jnp.concatenate(
        [grad_rot_queries, grad_rot_keys, pair_sums[:, key_width:]], axis=1
    ).astype(jnp.bfloat16)
    grad_mix = jnp.einsum(
        "nd,nf->df", normed_low, grad_projected, preferred_element_type=jnp.float32
    )
    grad_normed = jnp.einsum(
        "nf,df->nd", grad_projected, mix_full, preferred_element_type=jnp.float32
    )
    grad_gain_attn, grad_input_norm = norm_backward(grad_normed, unit_attn, scale_attn, gain_attn)
    grad_gains = jnp.stack([grad_gain_attn, grad_gain_mlp])
    attn_part = (
        lax.psum_scatter(grad_mix, ("seq", "fsdp"), scatter_dimension=0, tiled=True),
        lax.psum_scatter(grad_out, ("seq", "fsdp"), scatter_dimension=0, tiled=True),
        lax.psum_scatter(grad_gains, ("seq", "fsdp"), scatter_dimension=1, tiled=True),
    )
    return (grad_middle + grad_input_norm, attn_part, mlp_part)


def adam_update(weight, first, second, grad, clip_scale, rate):
    clipped = grad * clip_scale
    first_new = BETA_ONE * first + (1.0 - BETA_ONE) * clipped
    second_new = BETA_TWO * second + (1.0 - BETA_TWO) * clipped * clipped
    first_hat = first_new / (1.0 - BETA_ONE**STEP_NUMBER)
    second_hat = second_new / (1.0 - BETA_TWO**STEP_NUMBER)
    updated = weight - rate * (
        first_hat / (jnp.sqrt(second_hat) + EPS_ADAM) + WEIGHT_DECAY * weight
    )
    return (updated, first_new, second_new)


def local(
    tokens,
    cotangent,
    lengths,
    mix_weight,
    out_weight,
    in_weight,
    down_weight,
    norm_gains,
    mix_first,
    out_first,
    in_first,
    down_first,
    norm_first,
    mix_second,
    out_second,
    in_second,
    down_second,
    norm_second,
):
    row_count = tokens.shape[0]
    group_index = lax.axis_index("fsdp")
    cycle_index = lax.axis_index("seq")
    doc_lens = lax.dynamic_index_in_dim(lengths, group_index, 0, keepdims=False)
    query_places = cycle_index * row_count + jnp.arange(row_count, dtype=jnp.int32)
    query_segment, positions = doc_layout(query_places, doc_lens)
    keep_rows = (query_segment < doc_lens.shape[0]).astype(jnp.float32)[:, None]
    context = (query_places, query_segment, positions, keep_rows, doc_lens)
    stream = tokens.astype(jnp.float32)
    layer_index = 0
    attn_set, mlp_set = fetch_layer(
        mix_weight, out_weight, norm_gains, in_weight, down_weight, layer_index
    )
    stream, saved = layer_forward(stream, attn_set, mlp_set, context)
    saved_list = [saved]
    weight_list = [(attn_set, mlp_set)]
    hidden_out = stream.astype(jnp.bfloat16)
    grad_stream = cotangent.astype(jnp.float32)
    attn_sums = [None] * LAYERS
    mlp_sums = [None] * LAYERS
    for layer_index in reversed(range(LAYERS)):
        attn_set, mlp_set = weight_list[layer_index]
        grad_stream, attn_part, mlp_part = layer_backward(
            grad_stream, saved_list[layer_index], attn_set, mlp_set, context
        )
        attn_sums[layer_index] = attn_part
        mlp_sums[layer_index] = mlp_part
    mix_grad = jnp.stack([attn_sums[0][0]])
    out_grad = jnp.stack([attn_sums[0][1]])
    norm_grad = jnp.stack([attn_sums[0][2]])
    in_grad = jnp.stack([mlp_sums[0][0]])
    down_grad = jnp.stack([mlp_sums[0][1]])
    squares = (
        jnp.sum(mix_grad * mix_grad)
        + jnp.sum(out_grad * out_grad)
        + jnp.sum(in_grad * in_grad)
        + jnp.sum(down_grad * down_grad)
        + jnp.sum(norm_grad * norm_grad)
    )
    total_squares = lax.psum(squares, ("seq", "fsdp"))
    grad_norm = jnp.sqrt(total_squares)
    clip_scale = CLIP_NORM / jnp.maximum(grad_norm, CLIP_NORM)
    mix_new, mix_moment, mix_square = adam_update(
        mix_weight, mix_first, mix_second, mix_grad, clip_scale, LEARN_RATE
    )
    out_new, out_moment, out_square = adam_update(
        out_weight, out_first, out_second, out_grad, clip_scale, OUT_RATE
    )
    in_new, in_moment, in_square = adam_update(
        in_weight, in_first, in_second, in_grad, clip_scale, LEARN_RATE
    )
    down_new, down_moment, down_square = adam_update(
        down_weight, down_first, down_second, down_grad, clip_scale, LEARN_RATE
    )
    norm_new, norm_moment, norm_square = adam_update(
        norm_gains, norm_first, norm_second, norm_grad, clip_scale, GAIN_RATE
    )
    return (
        hidden_out,
        grad_stream,
        grad_norm,
        mix_grad,
        mix_new,
        mix_moment,
        mix_square,
        mix_new.astype(jnp.bfloat16),
        out_grad,
        out_new,
        out_moment,
        out_square,
        out_new.astype(jnp.bfloat16),
        in_grad,
        in_new,
        in_moment,
        in_square,
        in_new.astype(jnp.bfloat16),
        down_grad,
        down_new,
        down_moment,
        down_square,
        down_new.astype(jnp.bfloat16),
        norm_grad,
        norm_new,
        norm_moment,
        norm_square,
        norm_new.astype(jnp.bfloat16),
    )


def solution(mesh):
    return jax.shard_map(
        local,
        mesh=mesh,
        in_specs=(
            P(("seq", "fsdp"), None),
            P(("seq", "fsdp"), None),
            P(),
            P(None, ("seq", "fsdp"), None),
            P(None, ("seq", "fsdp"), None),
            P(None, ("seq", "fsdp"), None),
            P(None, ("seq", "fsdp"), None),
            P(None, None, ("seq", "fsdp")),
            P(None, ("seq", "fsdp"), None),
            P(None, ("seq", "fsdp"), None),
            P(None, ("seq", "fsdp"), None),
            P(None, ("seq", "fsdp"), None),
            P(None, None, ("seq", "fsdp")),
            P(None, ("seq", "fsdp"), None),
            P(None, ("seq", "fsdp"), None),
            P(None, ("seq", "fsdp"), None),
            P(None, ("seq", "fsdp"), None),
            P(None, None, ("seq", "fsdp")),
        ),
        out_specs=(
            P(("seq", "fsdp"), None),
            P(("seq", "fsdp"), None),
            P(),
            P(None, ("seq", "fsdp"), None),
            P(None, ("seq", "fsdp"), None),
            P(None, ("seq", "fsdp"), None),
            P(None, ("seq", "fsdp"), None),
            P(None, ("seq", "fsdp"), None),
            P(None, ("seq", "fsdp"), None),
            P(None, ("seq", "fsdp"), None),
            P(None, ("seq", "fsdp"), None),
            P(None, ("seq", "fsdp"), None),
            P(None, ("seq", "fsdp"), None),
            P(None, ("seq", "fsdp"), None),
            P(None, ("seq", "fsdp"), None),
            P(None, ("seq", "fsdp"), None),
            P(None, ("seq", "fsdp"), None),
            P(None, ("seq", "fsdp"), None),
            P(None, ("seq", "fsdp"), None),
            P(None, ("seq", "fsdp"), None),
            P(None, ("seq", "fsdp"), None),
            P(None, ("seq", "fsdp"), None),
            P(None, ("seq", "fsdp"), None),
            P(None, None, ("seq", "fsdp")),
            P(None, None, ("seq", "fsdp")),
            P(None, None, ("seq", "fsdp")),
            P(None, None, ("seq", "fsdp")),
            P(None, None, ("seq", "fsdp")),
        ),
        check_vma=False,
    )
```

profile of v0, /device:TPU:0, one launch (start us, length us, event | category | flops | bytes accessed | tf_op | source)
XLA Modules:
  0.0 1999.4 jit_solution(10162998748537187482)
XLA Ops:
  10.0 78.0 %all-gather = bf16[1,2,1536]{1,0,2:T(2,128)(2,1)S(1)} all-gather(bf16[1,2,48]{1,0,2:T(2,128)(2,1)S(1)} %copy.115), channel_id=2, replica_groups=mesh['seq'=16,'fsdp'=2] {'seq','fsdp'}, dimensions={2}, use_global_device_ids=true | all-gather | bytes 6336 | tf_op jit(solution)/shard_map/all_gather | solution.py:122
  89.2 25.1 %fusion.85 = (f32[1536]{0:T(1024)S(1)}, f32[1536]{0:T(1024)S(1)}) fusion(bf16[1,2,1536]{1,0,2:T(2,128)(2,1)S(1)} %all-gather), kind=kLoop, calls=%fused_computation.105 | loop fusion | flops 3072 | bytes 18432 | tf_op jit(solution)/shard_map/mul | solution.py:52
  114.4 5.2 fusion.48
  130.1 32.6 %all-gather.14.cloned.1.call-done = bf16[2048,768]{1,0:T(8,128)(2,1)} async-done(((bf16[128,768]{1,0:T(8,128)(2,1)}), bf16[2048,768]{1,0:T(8,128)(2,1)}) %all-gather.14.cloned.1.call-update) | async-done | bytes 3145744 | tf_op jit(solution)/shard_map/all_gather | solution.py:163
  162.7 4.7 copy.118
  167.4 44.1 %all-gather.12.cloned.1.call-done = bf16[2048,768]{0,1:T(8,128)(2,1)} async-done(((bf16[128,768]{0,1:T(8,128)(2,1)}), bf16[2048,768]{0,1:T(8,128)(2,1)}) %all-gather.12.cloned.1.call-update) | async-done | bytes 3145744 | tf_op jit(solution)/shard_map/all_gather | solution.py:162
  211.4 45.1 %while.32 = (s32[]{:T(128)}, f32[128,8,2]{0,2,1:T(2,128)S(1)}, f32[128,8,2]{0,2,1:T(2,128)S(1)}, f32[128,8,2,96]{0,3,2,1:T(8,128)S(1)}, s32[128]{0:T(128)S(1)}, ...) while((s32[]{:T(128)}, f32[128,8,2]{0,2,1:T(2,128)S(1)}, ...), condition=%wide.region_9.10_spmd.clone, body=%wide.region_5.0_spmd.clone.sunk | while | flops 417089152 | bytes 36450068 | solution.py:110
  215.1 2.8 fusion.162
  218.0 3.3 fusion.164
  226.5 2.8 fusion.162
  229.3 3.4 fusion.164
  237.8 2.8 fusion.162
  240.6 3.3 fusion.164
  249.1 2.8 fusion.162
  251.9 3.3 fusion.164
  257.0 19.7 all-gather.18.cloned.1.call-done
  276.6 3.3 multiply_reduce_fusion.5
  280.7 152.8 %all-gather.20.cloned.1.call-done = bf16[1,1536,8192]{2,1,0:T(8,128)(2,1)} async-done(((bf16[1,48,8192]{2,1,0:T(8,128)(2,1)}), bf16[1,1536,8192]{2,1,0:T(8,128)(2,1)}) %all-gather.20.cloned.1.call-update) | async-done | bytes 25165840 | tf_op jit(solution)/shard_map/all_gather | solution.py:125
  433.4 13.7 fusion.40
  447.1 83.8 %all-gather.22.cloned.1.call-done = bf16[1,4096,1536]{2,1,0:T(8,128)(2,1)} async-done(((bf16[1,128,1536]{2,1,0:T(8,128)(2,1)}), bf16[1,4096,1536]{2,1,0:T(8,128)(2,1)}) %all-gather.22.cloned.1.call-update) | async-done | bytes 12582928 | tf_op jit(solution)/shard_map/all_gather | solution.py:128
  531.0 11.8 multiply_convert_fusion.1
  542.7 14.7 multiply_reduce_fusion.1
  558.6 4.0 fusion.66
  565.3 77.4 %while.33 = (s32[]{:T(128)}, f32[128,8,2,96]{0,3,2,1:T(8,128)}, f32[4,512,1536]{2,1,0:T(8,128)}, s32[4]{0:T(128)S(1)}, bf16[2048,768]{0,1:T(8,128)(2,1)}, /*inde...) while((s32[]{:T(128)}, f32[128,8,2,96]{0,3,2,1:T(8,128)}, ...), condition=%wide.region_15.16_spmd.clone, body=%wide.region_13.15_spmd.clone.sunk | while | flops 1020993152 | bytes 83333112 | solution.py:312
  569.8 3.0 fusion.178
  575.3 2.2 fusion.180
  578.2 1.9 maximum_bitcast_fusion.2
  580.2 2.4 copy.151
  589.0 3.0 fusion.178
  592.0 2.7 fusion.179
  594.7 2.2 fusion.180
  597.7 1.9 maximum_bitcast_fusion.2
  599.6 2.4 copy.151
  602.0 1.9 constant_dynamic-update-slice_fusion.2
  608.4 3.0 fusion.178
  611.5 2.7 fusion.179
  614.2 2.2 fusion.180
  617.1 1.9 maximum_bitcast_fusion.2
  619.1 2.4 copy.151
  627.8 3.0 fusion.178
  630.8 2.7 fusion.179
  633.5 2.2 fusion.180
  636.5 1.9 maximum_bitcast_fusion.2
  638.4 2.4 copy.151
  642.7 12.7 copy.123
  656.8 6.0 fusion.92
  664.3 124.3 %reduce-scatter.9.cloned.1.call-done = f32[128,1536]{0,1:T(8,128)} async-done(((f32[2048,1536]{0,1:T(8,128)}), f32[128,1536]{0,1:T(8,128)}) %reduce-scatter.9.cloned.1.call-update) | async-done | bytes 786448 | tf_op jit(solution)/shard_map/reduce_scatter | solution.py:316
  790.8 8.0 fusion.81
  800.1 11.1 fusion.116
  811.2 9.4 fusion.89
  821.8 22.3 %fusion.71 = f32[1536,8192]{1,0:T(8,128)} fusion(bf16[128,4096]{1,0:T(8,128)(2,1)} %get-tuple-element.625, bf16[128,4096]{1,0:T(8,128)(2,1)} %get-tuple-element.624, f32[128,1536]{1,0:T(8,128)S(1)} %copy-done.7, f32[1536]{0:T(1024)S(1)} %get-tuple-element.544, f32[128]{0:T(128)S(1)} %copy-done.41), kind=kOutput, calls=%fused_computation.86 | convolution fusion | flops 3226009600 | bytes 53221888 | tf_op jit(solution)/shard_map/nd,nf->df/dot_general | solution.py:239
  844.1 8.0 fusion.63
  852.1 77.8 %reduce-scatter.13.cloned.1.call-done = f32[48,1536]{1,0:T(8,128)} async-done(((f32[1536,1536]{1,0:T(8,128)}), f32[48,1536]{1,0:T(8,128)}) %reduce-scatter.13.cloned.1.call-update) | async-done | bytes 294928 | tf_op jit(solution)/shard_map/reduce_scatter | solution.py:336
  931.5 99.3 %reduce-scatter.19.cloned.1.call-done = f32[48,2]{1,0:T(8,128)} async-done(((f32[1536,2]{1,0:T(8,128)}), f32[48,2]{1,0:T(8,128)}) %reduce-scatter.19.cloned.1.call-update) | async-done | bytes 400
  1032.3 251.1 %reduce-scatter.17.cloned.1.call-done = f32[128,1536]{1,0:T(8,128)} async-done(((f32[4096,1536]{1,0:T(8,128)}), f32[128,1536]{1,0:T(8,128)}) %reduce-scatter.17.cloned.1.call-update) | async-done | bytes 786448 | tf_op jit(solution)/shard_map/reduce_scatter | solution.py:247
  1283.4 1.9 multiply_reduce_fusion.2
  1285.3 211.5 %reduce-scatter.11.cloned.1.call-done = f32[48,3072]{1,0:T(8,128)} async-done(((f32[1536,3072]{1,0:T(8,128)}), f32[48,3072]{1,0:T(8,128)}) %reduce-scatter.11.cloned.1.call-update) | async-done | bytes 589840 | tf_op jit(solution)/shard_map/reduce_scatter | solution.py:335
  1500.0 434.2 %reduce-scatter.15.cloned.1.call-done = f32[48,8192]{1,0:T(8,128)} async-done(((f32[1536,8192]{1,0:T(8,128)}), f32[48,8192]{1,0:T(8,128)}) %reduce-scatter.15.cloned.1.call-update) | async-done | bytes 1572880 | tf_op jit(solution)/shard_map/reduce_scatter | solution.py:246
  1934.2 2.4 multiply_reduce_fusion
  1938.6 2.4 fusion.80
  1941.0 39.0 %psum.7 = f32[]{:T(128)} all-reduce(f32[]{:T(128)S(6)} %add.261), channel_id=1, replica_groups=mesh['seq'=16,'fsdp'=2] {'seq','fsdp'}, use_global_device_ids=true, to_apply=%region_30.31 | all-reduce | flops 1 | bytes 8 | tf_op jit(solution)/shard_map/psum | solution.py:413
  1981.4 3.0 fusion.113
  1985.7 3.3 fusion.109
  1989.0 2.0 fusion.107
  (299 shorter events, 77.4 us)
Async XLA Ops:
  7.2 114.3 %copy-start = (s32[2,5]{1,0:T(2,128)S(1)}, s32[2,5]{1,0:T(2,128)}, u32[]{:S(2)}) copy-start(s32[2,5]{1,0:T(2,128)} %param.24) | copy-start | bytes 124
  7.2 107.2 %copy-start.10 = (bf16[128,1536]{1,0:T(8,128)(2,1)S(1)}, bf16[128,1536]{1,0:T(8,128)(2,1)}, u32[]{:S(2)}) copy-start(bf16[128,1536]{1,0:T(8,128)(2,1)} %param.22) | copy-start | bytes 1179652
  7.2 107.1 %all-gather.16.cloned.1.call-start = ((), (), s32[]{:S(2)}) async-start(), calls=%async_computation.13 | async-start | bytes 9732096 | tf_op jit(solution)/shard_map/all_gather | solution.py:116
  9.2 153.5 %all-gather.14.cloned.1.call-start = ((), (), s32[]{:S(2)}) async-start(), calls=%async_computation.7 | async-start | bytes 3342336 | tf_op jit(solution)/shard_map/all_gather | solution.py:163
  89.2 30.4 %copy-start.42 = (f32[128]{0:T(128)}, f32[128]{0:T(128)S(1)}, u32[]{:S(2)}) copy-start(f32[128]{0:T(128)S(1)} %add_rsqrt_fusion.1) | copy-start | bytes 1540
  114.3 5.2 copy-start.36
  120.7 3.9 copy-start.27
  120.7 4.7 copy-start.14
  121.4 90.0 %all-gather.12.cloned.1.call-start = ((), (), s32[]{:S(2)}) async-start(), calls=%async_computation.6 | async-start | bytes 3342336 | tf_op jit(solution)/shard_map/all_gather | solution.py:162
  122.6 7.3 copy-start.32
  124.6 152.0 %all-gather.18.cloned.1.call-start = ((), (), s32[]{:S(2)}) async-start(), calls=%async_computation.14 | async-start | bytes 4866048 | tf_op jit(solution)/shard_map/all_gather | solution.py:119
  125.4 4.3 slice-start
  125.4 308.1 %all-gather.20.cloned.1.call-start = ((), (), s32[]{:S(2)}) async-start(), calls=%async_computation.15 | async-start | bytes 25952256 | tf_op jit(solution)/shard_map/all_gather | solution.py:125
  126.4 404.5 %all-gather.22.cloned.1.call-start = ((), (), s32[]{:S(2)}) async-start(), calls=%async_computation.16 | async-start | bytes 12976128 | tf_op jit(solution)/shard_map/all_gather | solution.py:128
  128.4 660.2 %reduce-scatter.9.cloned.1.call-start = ((), (), s32[]{:S(2)}) async-start(), calls=%async_computation.8 | async-start | bytes 13369344 | tf_op jit(solution)/shard_map/reduce_scatter | solution.py:316
  129.7 433.9 %copy-start.44 = (f32[128]{0:T(128)}, f32[128]{0:T(128)S(1)}, u32[]{:S(2)}) copy-start(f32[128]{0:T(128)S(1)} %compare_convert_fusion.1) | copy-start | bytes 1540
  218.0 3.5 copy-start.2
  229.3 3.5 copy-start.2
  240.6 3.5 copy-start.2
  251.9 3.4 copy-start.2
  257.0 23.0 %copy-start.12 = (f32[128,1536]{1,0:T(8,128)}, f32[128,1536]{1,0:T(8,128)S(1)}, u32[]{:S(2)}) copy-start(f32[128,1536]{1,0:T(8,128)S(1)} %copy.119) | copy-start | bytes 2359300
  279.9 277.5 %copy-start.6 = (f32[128,1536]{1,0:T(8,128)}, f32[128,1536]{1,0:T(8,128)S(1)}, u32[]{:S(2)}) copy-start(f32[128,1536]{1,0:T(8,128)S(1)} %get-tuple-element.639) | copy-start | bytes 2359300
  279.9 277.5 %copy-start.40 = (f32[128]{0:T(128)}, f32[128]{0:T(128)S(1)}, u32[]{:S(2)}) copy-start(f32[128]{0:T(128)S(1)} %add_rsqrt_fusion) | copy-start | bytes 1540
  433.4 97.5 %copy-start.25 = (bf16[128,1536]{1,0:T(8,128)(2,1)S(1)}, bf16[128,1536]{1,0:T(8,128)(2,1)}, u32[]{:S(2)}) copy-start(bf16[128,1536]{1,0:T(8,128)(2,1)} %param.23) | copy-start | bytes 1179652
  565.3 3.5 copy-start.51
  568.8 4.0 copy-start.3
  584.5 3.5 copy-start.51
  588.0 4.0 copy-start.3
  592.0 2.7 copy-start.4
  603.9 3.5 copy-start.51
  607.4 4.0 copy-start.3
  623.3 3.5 copy-start.51
  626.8 4.0 copy-start.3
  630.8 2.7 copy-start.4
  655.4 274.4 %reduce-scatter.13.cloned.1.call-start = ((), (), s32[]{:S(2)}) async-start(), calls=%async_computation.10 | async-start | bytes 9732096 | tf_op jit(solution)/shard_map/reduce_scatter | solution.py:336
  662.8 128.0 %copy-start.11 = (bf16[128,1536]{1,0:T(8,128)(2,1)S(1)}, bf16[128,1536]{1,0:T(8,128)(2,1)}, u32[]{:S(2)}) copy-start(bf16[128,1536]{1,0:T(8,128)(2,1)} %param.22) | copy-start | bytes 1179652
  662.8 128.0 %copy-start.37 = (f32[1536]{0:T(1024)S(1)}, f32[1536]{0:T(1024)}, u32[]{:S(2)}) copy-start(f32[1536]{0:T(1024)} %copy-done.36) | copy-start | bytes 18436
  662.8 128.0 %copy-start.43 = (f32[128]{0:T(128)S(1)}, f32[128]{0:T(128)}, u32[]{:S(2)}) copy-start(f32[128]{0:T(128)} %copy-done.42) | copy-start | bytes 1540
  662.8 368.0 %reduce-scatter.19.cloned.1.call-start = ((), (), s32[]{:S(2)}) async-start(), calls=%async_computation.17 | async-start | bytes 811008
  790.8 8.0 copy-start.39
  790.8 9.3 copy-start.17
  790.8 9.3 copy-start.26
  800.0 483.3 %reduce-scatter.17.cloned.1.call-start = ((), (), s32[]{:S(2)}) async-start(), calls=%async_computation.12 | async-start | bytes 25952256 | tf_op jit(solution)/shard_map/reduce_scatter | solution.py:247
  811.2 685.6 %reduce-scatter.11.cloned.1.call-start = ((), (), s32[]{:S(2)}) async-start(), calls=%async_computation.9 | async-start | bytes 19464192 | tf_op jit(solution)/shard_map/reduce_scatter | solution.py:335
  820.6 1113.5 %reduce-scatter.15.cloned.1.call-start = ((), (), s32[]{:S(2)}) async-start(), calls=%async_computation.11 | async-start | bytes 51904512 | tf_op jit(solution)/shard_map/reduce_scatter | solution.py:246
  852.1 1128.7 %copy-start.48 = (f32[1,2,48]{2,1,0:T(2,128)S(1)}, f32[1,2,48]{2,1,0:T(2,128)}, u32[]{:S(2)}) copy-start(f32[1,2,48]{2,1,0:T(2,128)} %param.29) | copy-start | bytes 1156
  852.1 1128.7 %copy-start.49 = (f32[1,2,48]{2,1,0:T(2,128)S(1)}, f32[1,2,48]{2,1,0:T(2,128)}, u32[]{:S(2)}) copy-start(f32[1,2,48]{2,1,0:T(2,128)} %param.34) | copy-start | bytes 1156
  852.1 1128.7 %copy-start.50 = (f32[1,2,48]{2,1,0:T(2,128)S(1)}, f32[1,2,48]{2,1,0:T(2,128)}, u32[]{:S(2)}) copy-start(f32[1,2,48]{2,1,0:T(2,128)} %param.39) | copy-start | bytes 1156
  852.1 1129.3 %copy-start.21 = (f32[1,48,3072]{2,1,0:T(8,128)S(1)}, f32[1,48,3072]{2,1,0:T(8,128)}, u32[]{:S(2)}) copy-start(f32[1,48,3072]{2,1,0:T(8,128)} %param.25) | copy-start | bytes 1769476
  1031.6 952.8 %copy-start.47 = (f32[2,48]{1,0:T(2,128)}, f32[2,48]{1,0:T(2,128)S(1)}, u32[]{:S(2)}) copy-start(f32[2,48]{1,0:T(2,128)S(1)} %copy.135) | copy-start | bytes 1156
  1496.8 484.6 %copy-start.22 = (f32[48,3072]{1,0:T(8,128)S(1)}, f32[48,3072]{1,0:T(8,128)}, u32[]{:S(2)}) copy-start(f32[48,3072]{1,0:T(8,128)} %reduce-scatter.11.cloned.1.call-done) | copy-start | bytes 1769476
  1938.5 45.9 %copy-start.28 = (f32[1,48,1536]{2,1,0:T(8,128)S(1)}, f32[1,48,1536]{2,1,0:T(8,128)}, u32[]{:S(2)}) copy-start(f32[1,48,1536]{2,1,0:T(8,128)} %param.26) | copy-start | bytes 884740
  1938.6 45.9 %copy-start.29 = (f32[48,1536]{1,0:T(8,128)S(1)}, f32[48,1536]{1,0:T(8,128)}, u32[]{:S(2)}) copy-start(f32[48,1536]{1,0:T(8,128)} %reduce-scatter.13.cloned.1.call-done) | copy-start | bytes 884740
  1938.6 45.9 %copy-start.34 = (f32[1,48,1536]{2,1,0:T(8,128)S(1)}, f32[1,48,1536]{2,1,0:T(8,128)}, u32[]{:S(2)}) copy-start(f32[1,48,1536]{2,1,0:T(8,128)} %param.31) | copy-start | bytes 884740
  1941.0 43.5 %copy-start.35 = (f32[1,48,1536]{2,1,0:T(8,128)S(1)}, f32[1,48,1536]{2,1,0:T(8,128)}, u32[]{:S(2)}) copy-start(f32[1,48,1536]{2,1,0:T(8,128)} %param.36) | copy-start | bytes 884740
  1981.4 4.2 copy-start.15
  1981.4 4.2 copy-start.16
  1981.4 4.2 copy-start.23
  1981.4 4.2 copy-start.24
  1985.6 3.4 copy-start.19
  1985.7 3.3 copy-start.20
  1985.7 3.3 copy-start.30
  1985.7 3.3 copy-start.31
  1985.7 5.3 copy-start.1
  (17 other events, 25.8 us)
Sparse Core Ops, SparseCore 0:
  11.6 88.7 all-gather.15
  121.6 41.0 all-gather.13
  165.4 46.0 all-gather.11
  214.8 61.7 all-gather.17
  279.9 153.4 all-gather.19
  436.7 94.1 all-gather.21
  655.6 133.0 reduce-scatter.8
  795.1 134.7 reduce-scatter.12
  936.3 94.4 reduce-scatter.18
  1038.8 244.5 reduce-scatter.16
  1290.4 206.3 reduce-scatter.10
  1503.6 430.5 reduce-scatter.14
where the time goes:
time: 2010 us; the launch traced here: 2000 us
  waiting for transfers between devices  1530 us (76%)
  matrix products  170 us (8%)
  blocking collectives  117 us (6%)
  other arithmetic  88.1 us (4%)
  local copies, waits for them, and re-layouts  65.3 us (3%)
  between operations  20.5 us (1%)
    reduce_scatter x1, waiting for transfers between devices, layer_backward(): lax.psum_scatter(grad_in, ('seq', 'fsdp'), scatter_dimension=0, tiled=True)  434 us
    reduce_scatter x1, waiting for transfers between devices, layer_backward(): lax.psum_scatter(grad_down, ('seq', 'fsdp'), scatter_dimension=0, tiled=T...  251 us
    reduce_scatter x1, waiting for transfers between devices, layer_backward(): lax.psum_scatter(grad_mix, ('seq', 'fsdp'), scatter_dimension=0, tiled=True)  211 us
    all_gather x1, waiting for transfers between devices, fetch_layer(): lax.all_gather(in_weight[layer_index].astype(jnp.bfloat16), ('seq', 'fsdp...  153 us
    reduce_scatter x1, waiting for transfers between devices, layer_backward(): lax.psum_scatter(pair_terms, 'seq', scatter_dimension=0, tiled=True)  124 us
    unnamed x13, waiting for transfers between devices  99.5 us
    all_gather x1, waiting for transfers between devices, fetch_layer(): lax.all_gather(down_weight[layer_index].astype(jnp.bfloat16), ('seq', 'fs...  83.8 us
    all_gather x1, blocking collectives, fetch_layer(): lax.all_gather(norm_gains[layer_index].astype(jnp.bfloat16), ('seq', 'fsd...  78 us
  transfers between devices with their start and end apart: 12, of which 11 were waited for; matrix products, arithmetic and copies ran while one was open for 9% of the time, Pallas kernels for 0%

commit v1 on v0

--- a/solution.py
+++ b/solution.py
@@ -1,6 +1,8 @@
 import jax
 import jax.numpy as jnp
 from jax import lax
+from jax.experimental import pallas as pl
+from jax.experimental.pallas import tpu as pltpu
 from jax.sharding import PartitionSpec as P
 
 D = 1536
@@ -460,9 +462,803 @@
     )
 
 
+MESH = pl.DeviceIdType.MESH
+ANY = pl.BlockSpec(memory_space=pl.ANY)
+VMEM = pl.BlockSpec(memory_space=pltpu.VMEM)
+LOW = jnp.bfloat16
+SQUARE = 8
+SEQ = 16
+FLEET = 32
+ROWS = 128
+HALF_ROWS = 64
+KEYS = 1024
+BLOCK = 256
+CORE, NEAR_Y, NEAR_Z = 1, 2, 4
+LOG2E = 1.4426950408889634
+SCALE2 = HEAD_DIM ** (-0.5) * LOG2E
+WALL = 2.0**100
+
+
+def flip(value, bits):
+    for bit in (1, 2, 4, 8):
+        if bits & bit:
+            value = value + bit - 2 * bit * (lax.rem(lax.div(value, bit), 2))
+    return value
+
+
+class Place:
+    def __init__(self):
+        self.seq = lax.axis_index("seq")
+        self.fsdp = lax.axis_index("fsdp")
+        self.member = lax.rem(self.seq, SQUARE)
+        self.half = lax.div(self.seq, SQUARE)
+        self.rank = self.seq * 2 + self.fsdp
+
+    def peer(self, bits):
+        return (flip(self.seq, bits), self.fsdp)
+
+    def slot(self, bits):
+        return flip(self.member, bits)
+
+    def after(self, step):
+        rank = lax.rem(self.rank + step, FLEET)
+        return rank, (lax.div(rank, 2), lax.rem(rank, 2))
+
+    def before(self, step):
+        return lax.rem(self.rank + FLEET - step, FLEET)
+
+
+def send(src, dst, sems, index, device):
+    return pltpu.make_async_remote_copy(
+        src_ref=src,
+        dst_ref=dst,
+        send_sem=sems[0].at[index],
+        recv_sem=sems[1].at[index],
+        device_id=device,
+        device_id_type=MESH,
+    )
+
+
+def greet(devices):
+    barrier = pltpu.get_barrier_semaphore()
+    for device in devices:
+        pl.semaphore_signal(barrier, inc=1, device_id=device, device_id_type=MESH)
+    pl.semaphore_wait(barrier, len(devices))
+
+
+def pair_sems(count):
+    return [pltpu.SemaphoreType.DMA((count,)), pltpu.SemaphoreType.DMA((count,))]
+
+
+class SquareGather:
+    COPIES = 10
+
+    def __init__(self, place, src, out, sems, local_sem):
+        p, h = place, HALF_ROWS
+        own, ys, zs = p.slot(0), p.slot(NEAR_Y), p.slot(NEAR_Z)
+        ds = p.slot(NEAR_Y | NEAR_Z)
+        to_y, to_z, to_c = p.peer(NEAR_Y), p.peer(NEAR_Z), p.peer(CORE)
+        top, low = pl.ds(0, h), pl.ds(h, h)
+        self.local = pltpu.make_async_copy(src, out.at[own], local_sem)
+        self.y0 = send(src.at[top], out.at[own, top], sems, 0, to_y)
+        self.y1 = send(src.at[low], out.at[own, low], sems, 1, to_y)
+        self.z1 = send(src.at[low], out.at[own, low], sems, 2, to_z)
+        self.z0 = send(src.at[top], out.at[own, top], sems, 3, to_z)
+        self.fz = send(out.at[ys, top], out.at[ys, top], sems, 4, to_z)
+        self.fy = send(out.at[zs, low], out.at[zs, low], sems, 5, to_y)
+        self.c = [
+            send(src, out.at[own], sems, 6, to_c),
+            send(out.at[ys], out.at[ys], sems, 7, to_c),
+            send(out.at[zs], out.at[zs], sems, 8, to_c),
+            send(out.at[ds], out.at[ds], sems, 9, to_c),
+        ]
+
+    def start(self):
+        for copy in (self.y0, self.z1, self.y1, self.z0, self.c[0], self.local):
+            copy.start()
+
+    def relay(self):
+        self.y0.wait_recv()
+        self.fz.start()
+        self.z1.wait_recv()
+        self.fy.start()
+
+    def share(self):
+        self.y1.wait_recv()
+        self.c[1].start()
+        self.z0.wait_recv()
+        self.c[2].start()
+
+    def finish(self):
+        self.fz.wait_recv()
+        self.fy.wait_recv()
+        self.c[3].start()
+        for copy in self.c:
+            copy.wait_recv()
+        for copy in [self.y0, self.y1, self.z0, self.z1, self.fz, self.fy] + self.c:
+            copy.wait_send()
+        self.local.wait()
+
+
+def first_kernel(tok, cot, gain, mix, inn, out, tok_o, cot_o, gain_o, mix_o, inn_o, out_o, *sems):
+    place = Place()
+    tok_s, cot_s, gain_s, mix_s, inn_s, out_s = (sems[2 * i : 2 * i + 2] for i in range(6))
+    local_sem = sems[12]
+    greet([place.after(step)[1] for step in range(1, FLEET)])
+    gather_tok = SquareGather(place, tok, tok_o, tok_s, local_sem.at[0])
+    gather_cot = SquareGather(place, cot, cot_o, cot_s, local_sem.at[1])
+    gather_tok.start()
+    copies = []
+    for step in range(1, FLEET):
+        rank, device = place.after(step)
+        column = lax.rem(device[0], SQUARE)
+        copies.append(send(gain, gain_o.at[place.rank], gain_s, step, device))
+        copies.append(send(mix.at[column], mix_o.at[place.rank], mix_s, step, device))
+    locals_ = [
+        pltpu.make_async_copy(gain, gain_o.at[place.rank], local_sem.at[2]),
+        pltpu.make_async_copy(mix.at[place.member], mix_o.at[place.rank], local_sem.at[3]),
+        pltpu.make_async_copy(inn.at[place.member], inn_o.at[place.member], local_sem.at[4]),
+    ]
+    for bits in range(1, SQUARE):
+        copies.append(
+            send(inn.at[place.slot(bits)], inn_o.at[place.member], inn_s, bits, place.peer(bits))
+        )
+    for copy in copies + locals_:
+        copy.start()
+    keeper = lax.div(place.seq, 2)
+    spot = lax.rem(place.seq, 2) * 2 + place.fsdp
+
+    def out_copy(number):
+        device = ((number // 2) * SQUARE + keeper, number % 2)
+        remote = pltpu.make_async_remote_copy(
+            src_ref=out,
+            dst_ref=out_o.at[spot],
+            send_sem=out_s[0].at[number],
+            recv_sem=out_s[1].at[spot],
+            device_id=device,
+            device_id_type=MESH,
+        )
+        local = pltpu.make_async_copy(out, out_o.at[spot], local_sem.at[5])
+        mine = (device[0] == place.seq) & (device[1] == place.fsdp)
+        return remote, local, mine
+
+    for number in range(4):
+        remote, local, mine = out_copy(number)
+        pl.when(mine)(local.start)
+        pl.when(jnp.logical_not(mine))(remote.start)
+    gather_tok.relay()
+    gather_tok.share()
+    gather_cot.start()
+    gather_cot.relay()
+    gather_cot.share()
+    gather_tok.finish()
+    gather_cot.finish()
+    for copy in copies + locals_:
+        copy.wait()
+    for number in range(4):
+        remote, local, mine = out_copy(number)
+        pl.when(mine)(local.wait)
+        pl.when(jnp.logical_not(mine))(remote.wait_send)
+    for number in range(4):
+        source_seq = place.member * 2 + number // 2
+        mine = (source_seq == place.seq) & (number % 2 == place.fsdp)
+        arrival = pltpu.make_async_remote_copy(
+            src_ref=out,
+            dst_ref=out_o.at[number],
+            send_sem=out_s[0].at[number],
+            recv_sem=out_s[1].at[number],
+            device_id=(source_seq, number % 2),
+            device_id_type=MESH,
+        )
+        pl.when(jnp.logical_not(mine))(arrival.wait_recv)
+
+
+def first_exchange(tok, cot, gain, mix, inn, out):
+    shape = jax.ShapeDtypeStruct
+    return pl.pallas_call(
+        first_kernel,
+        out_shape=(
+            shape((SQUARE,) + tok.shape, LOW),
+            shape((SQUARE,) + cot.shape, LOW),
+            shape((FLEET,) + gain.shape, gain.dtype),
+            shape((FLEET,) + mix.shape[1:], LOW),
+            shape(inn.shape, LOW),
+            shape((4,) + out.shape, LOW),
+        ),
+        in_specs=[ANY] * 6,
+        out_specs=(ANY,) * 6,
+        scratch_shapes=pair_sems(SquareGather.COPIES)
+        + pair_sems(SquareGather.COPIES)
+        + pair_sems(FLEET)
+        + pair_sems(FLEET)
+        + pair_sems(SQUARE)
+        + pair_sems(4)
+        + [pltpu.SemaphoreType.DMA((6,))],
+        compiler_params=pltpu.CompilerParams(collective_id=0, has_side_effects=True),
+        name="first_exchange",
+    )(tok, cot, gain, mix, inn, out)
+
+
+def gather_kernel(src, out, send_sems, recv_sems, local_sem):
+    place = Place()
+    greet([place.peer(bits) for bits in (CORE, NEAR_Y, NEAR_Z)])
+    gather = SquareGather(place, src, out, (send_sems, recv_sems), local_sem.at[0])
+    gather.start()
+    gather.relay()
+    gather.share()
+    gather.finish()
+
+
+def square_gather(block):
+    return pl.pallas_call(
+        gather_kernel,
+        out_shape=jax.ShapeDtypeStruct((SQUARE,) + block.shape, block.dtype),
+        in_specs=[ANY],
+        out_specs=ANY,
+        scratch_shapes=pair_sems(SquareGather.COPIES) + [pltpu.SemaphoreType.DMA((1,))],
+        compiler_params=pltpu.CompilerParams(collective_id=1, has_side_effects=True),
+        name="square_gather",
+    )(block).reshape(SQUARE * block.shape[0], block.shape[1])
+
+
+def add_rows(target, left, right, start, count):
+    step = 16
+
+    def body(number, _):
+        rows = pl.ds(pl.multiple_of(start + number * step, step), step)
+        target[rows] = (left[rows].astype(jnp.float32) + right[rows].astype(jnp.float32)).astype(
+            target.dtype
+        )
+        return 0
+
+    lax.fori_loop(0, count // step, body, 0)
+
+
+def scatter_kernel(part, total, sib, away, passed, landed, send_sems, recv_sems):
+    place = Place()
+    sems = (send_sems, recv_sems)
+    greet([place.peer(bits) for bits in (CORE, NEAR_Y, NEAR_Z)])
+    h = HALF_ROWS
+    top, low = pl.ds(0, h), pl.ds(h, h)
+    far = NEAR_Y | NEAR_Z
+    to_y, to_z, to_c = place.peer(NEAR_Y), place.peer(NEAR_Z), place.peer(CORE)
+    cores = [
+        send(part.at[place.slot(bits | CORE)], sib.at[number], sems, number, to_c)
+        for number, bits in enumerate((far, NEAR_Y, NEAR_Z, 0))
+    ]
+    for copy in cores:
+        copy.start()
+    d0 = send(away.at[0, top], passed.at[top], sems, 4, to_y)
+    d1 = send(away.at[0, low], passed.at[low], sems, 5, to_z)
+    y0 = send(away.at[1, top], landed.at[0, top], sems, 6, to_y)
+    y1 = send(away.at[1, low], landed.at[0, low], sems, 7, to_y)
+    z0 = send(away.at[2, top], landed.at[1, top], sems, 8, to_z)
+    z1 = send(away.at[2, low], landed.at[1, low], sems, 9, to_z)
+    cores[0].wait_recv()
+    add_rows(away.at[0], part.at[place.slot(far)], sib.at[0], 0, ROWS)
+    d0.start()
+    d1.start()
+    cores[1].wait_recv()
+    add_rows(away.at[1], part.at[place.slot(NEAR_Y)], sib.at[1], 0, ROWS)
+    y0.start()
+    cores[2].wait_recv()
+    add_rows(away.at[2], part.at[place.slot(NEAR_Z)], sib.at[2], 0, ROWS)
+    z1.start()
+    cores[3].wait_recv()
+    add_rows(total, part.at[place.slot(0)], sib.at[3], 0, ROWS)
+    d0.wait_recv()
+    add_rows(away.at[2], away.at[2], passed, 0, h)
+    z0.start()
+    d1.wait_recv()
+    add_rows(away.at[1], away.at[1], passed, h, h)
+    y1.start()
+    y0.wait_recv()
+    z1.wait_recv()
+    add_rows(total, total, landed.at[0], 0, h)
+    add_rows(total, total, landed.at[1], h, h)
+    z0.wait_recv()
+    add_rows(total, total, landed.at[1], 0, h)
+    y1.wait_recv()
+    add_rows(total, total, landed.at[0], h, h)
+    for copy in cores + [d0, d1, y0, y1, z0, z1]:
+        copy.wait_send()
+
+
+def square_scatter(part):
+    width = part.shape[-1]
+    return pl.pallas_call(
+        scatter_kernel,
+        out_shape=jax.ShapeDtypeStruct((ROWS, width), jnp.float32),
+        in_specs=[VMEM],
+        out_specs=VMEM,
+        scratch_shapes=[
+            pltpu.VMEM((4, ROWS, width), LOW),
+            pltpu.VMEM((3, ROWS, width), LOW),
+            pltpu.VMEM((ROWS, width), LOW),
+            pltpu.VMEM((2, ROWS, width), LOW),
+        ]
+        + pair_sems(10),
+        compiler_params=pltpu.CompilerParams(
+            collective_id=2, has_side_effects=True, vmem_limit_bytes=32 << 20
+        ),
+        name="square_scatter",
+    )(part.reshape(SQUARE, ROWS, width))
+
+
+def last_kernel(inn, mix, out, gain, inn_o, mix_o, out_o, gain_o, *sems):
+    place = Place()
+    inn_s, mix_s, out_s, gain_s = (sems[2 * i : 2 * i + 2] for i in range(4))
+    local_sem = sems[8]
+    greet([place.after(step)[1] for step in range(1, FLEET)])
+    copies = []
+    for bits in range(1, SQUARE):
+        peer, slot = place.peer(bits), place.slot(bits)
+        copies.append(send(mix.at[slot], mix_o.at[place.member], mix_s, bits, peer))
+        copies.append(send(inn.at[slot], inn_o.at[place.member], inn_s, bits, peer))
+    for step in range(1, FLEET):
+        rank, device = place.after(step)
+        copies.append(send(gain.at[rank], gain_o.at[place.rank], gain_s, step, device))
+    copies += [
+        pltpu.make_async_copy(inn.at[place.member], inn_o.at[place.member], local_sem.at[0]),
+        pltpu.make_async_copy(mix.at[place.member], mix_o.at[place.member], local_sem.at[1]),
+        pltpu.make_async_copy(gain.at[place.rank], gain_o.at[place.rank], local_sem.at[2]),
+    ]
+    for copy in copies:
+        copy.start()
+
+    def out_copy(number):
+        owner = place.member * 2 + number
+        remote = pltpu.make_async_remote_copy(
+            src_ref=out.at[number],
+            dst_ref=out_o.at[place.half],
+            send_sem=out_s[0].at[number],
+            recv_sem=out_s[1].at[place.half],
+            device_id=(owner, place.fsdp),
+            device_id_type=MESH,
+        )
+        local = pltpu.make_async_copy(out.at[number], out_o.at[place.half], local_sem.at[3])
+        return remote, local, owner == place.seq
+
+    for number in range(2):
+        remote, local, mine = out_copy(number)
+        pl.when(mine)(local.start)
+        pl.when(jnp.logical_not(mine))(remote.start)
+    for copy in copies:
+        copy.wait()
+    for number in range(2):
+        remote, local, mine = out_copy(number)
+        pl.when(mine)(local.wait)
+        pl.when(jnp.logical_not(mine))(remote.wait_send)
+    for half in range(2):
+        source_seq = half * SQUARE + lax.div(place.seq, 2)
+        arrival = pltpu.make_async_remote_copy(
+            src_ref=out.at[0],
+            dst_ref=out_o.at[half],
+            send_sem=out_s[0].at[half],
+            recv_sem=out_s[1].at[half],
+            device_id=(source_seq, place.fsdp),
+            device_id_type=MESH,
+        )
+        pl.when(source_seq != place.seq)(arrival.wait_recv)
+
+
+def last_exchange(inn, mix, out, gain):
+    shape = jax.ShapeDtypeStruct
+    return pl.pallas_call(
+        last_kernel,
+        out_shape=tuple(shape(v.shape, v.dtype) for v in (inn, mix, out, gain)),
+        in_specs=[ANY] * 4,
+        out_specs=(ANY,) * 4,
+        scratch_shapes=pair_sems(SQUARE)
+        + pair_sems(SQUARE)
+        + pair_sems(2)
+        + pair_sems(FLEET)
+        + [pltpu.SemaphoreType.DMA((4,))],
+        compiler_params=pltpu.CompilerParams(collective_id=3, has_side_effects=True),
+        name="last_exchange",
+    )(inn, mix, out, gain)
+
+
+def share_kernel(value, out, send_sems, recv_sems):
+    place = Place()
+    greet([place.after(step)[1] for step in range(1, FLEET)])
+    out[place.rank] = value[...]
+    copies = []
+    for step in range(1, FLEET):
+        rank, device = place.after(step)
+        copies.append(send(value, out.at[place.rank], (send_sems, recv_sems), step, device))
+    for copy in copies:
+        copy.start()
+    for copy in copies:
+        copy.wait()
+
+
+def share_all(value):
+    return pl.pallas_call(
+        share_kernel,
+        out_shape=jax.ShapeDtypeStruct((FLEET,) + value.shape, value.dtype),
+        in_specs=[VMEM],
+        out_specs=VMEM,
+        scratch_shapes=pair_sems(FLEET),
+        compiler_params=pltpu.CompilerParams(collective_id=4, has_side_effects=True),
+        name="share_all",
+    )(value)
+
+
+def dot32(left, right, dims=((1,), (0,))):
+    return lax.dot_general(left, right, (dims, ((), ())), preferred_element_type=jnp.float32)
+
+
+def block_of(number):
+    return pl.ds(pl.multiple_of(number * BLOCK, BLOCK), BLOCK)
+
+
+def later(number_of_columns):
+    key_at = lax.broadcasted_iota(jnp.int32, (BLOCK, number_of_columns), 0)
+    query_at = lax.rem(lax.broadcasted_iota(jnp.int32, (BLOCK, number_of_columns), 1), BLOCK)
+    return key_at > query_at
+
+
+def attend_kernel(half, query_t, keys, values_t, out_t, log_sum):
+    first = jnp.where(half[0] == 1, 0, KEYS // BLOCK)
+    for number in range(KEYS // BLOCK):
+        columns = pl.ds(number * BLOCK, BLOCK)
+        queries = jnp.concatenate([query_t[0, :, columns], query_t[1, :, columns]], axis=1)
+
+        def fold(place, carry, diagonal=False):
+            score = dot32(keys[block_of(place), :], queries)
+            if diagonal:
+                score = jnp.where(later(2 * BLOCK), -WALL, score)
+            top = jnp.max(score, axis=0, keepdims=True)
+            if carry is not None:
+                top = jnp.maximum(carry[0], top)
+            weight = jnp.exp2((score - top) * SCALE2)
+            total = jnp.sum(weight, axis=0, keepdims=True)
+            mixed = dot32(values_t[:, block_of(place)], weight.astype(LOW))
+            if carry is not None:
+                fade = jnp.exp2((carry[0] - top) * SCALE2)
+                total = total + carry[1] * fade
+                mixed = mixed + carry[2] * fade
+            return (top, total, mixed)
+
+        last = KEYS // BLOCK + number
+        carry = fold(last, None, diagonal=True)
+        top, total, mixed = lax.fori_loop(first, last, fold, carry)
+        mixed = mixed * (1.0 / total)
+        level = top * SCALE2 + jnp.log2(total)
+        for head in range(2):
+            side = slice(head * BLOCK, (head + 1) * BLOCK)
+            out_t[head, :, columns] = mixed[:, side]
+            log_sum[pl.ds(head, 1), columns] = level[:, side]
+
+
+def attend(half, query_t, keys, values_t):
+    return pl.pallas_call(
+        attend_kernel,
+        out_shape=(
+            jax.ShapeDtypeStruct((2, HEAD_DIM, KEYS), jnp.float32),
+            jax.ShapeDtypeStruct((2, KEYS), jnp.float32),
+        ),
+        in_specs=[pl.BlockSpec(memory_space=pltpu.SMEM)] + [VMEM] * 3,
+        out_specs=(VMEM, VMEM),
+        compiler_params=pltpu.CompilerParams(vmem_limit_bytes=40 << 20),
+        name="attend",
+    )(half, query_t, keys, values_t)
+
+
+def attend_back_kernel(
+    half, query_t, queries_r, keys, keys_t, values, grad_t, grad_r, log_sum, delta, dq_t, dk, dv
+):
+    first = jnp.where(half[0] == 1, 0, KEYS // BLOCK)
+    dk[...] = jnp.zeros_like(dk)
+    dv[...] = jnp.zeros_like(dv)
+    for number in range(KEYS // BLOCK):
+        columns = pl.ds(number * BLOCK, BLOCK)
+
+        def both(ref, axis):
+            if axis == 1:
+                return jnp.concatenate([ref[0, :, columns], ref[1, :, columns]], axis=1)
+            return jnp.concatenate([ref[0, columns, :], ref[1, columns, :]], axis=0)
+
+        query_c, grad_c = both(query_t, 1), both(grad_t, 1)
+        query_b, grad_b = both(queries_r, 0), both(grad_r, 0)
+        level = jnp.concatenate([log_sum[0:1, columns], log_sum[1:2, columns]], axis=1)
+        shift = jnp.concatenate([delta[0:1, columns], delta[1:2, columns]], axis=1)
+
+        def fold(place, total, diagonal=False):
+            rows = block_of(place)
+            score = dot32(keys[rows, :], query_c)
+            if diagonal:
+                score = jnp.where(later(2 * BLOCK), -WALL, score)
+            weight = jnp.exp2(score * SCALE2 - level)
+            grad_weight = dot32(values[rows, :], grad_c)
+            grad_score = (weight * (grad_weight - shift)).astype(LOW)
+            dk[rows, :] += dot32(grad_score, query_b)
+            dv[rows, :] += dot32(weight.astype(LOW), grad_b)
+            return total + dot32(keys_t[:, rows], grad_score)
+
+        last = KEYS // BLOCK + number
+        total = fold(last, jnp.zeros((HEAD_DIM, 2 * BLOCK), jnp.float32), diagonal=True)
+        total = lax.fori_loop(first, last, fold, total)
+        for head in range(2):
+            dq_t[head, :, columns] = total[:, head * BLOCK : (head + 1) * BLOCK]
+
+
+def attend_back(half, *arrays):
+    shape = jax.ShapeDtypeStruct
+    return pl.pallas_call(
+        attend_back_kernel,
+        out_shape=(
+            shape((2, HEAD_DIM, KEYS), jnp.float32),
+            shape((2 * KEYS, HEAD_DIM), jnp.float32),
+            shape((2 * KEYS, HEAD_DIM), jnp.float32),
+        ),
+        in_specs=[pl.BlockSpec(memory_space=pltpu.SMEM)] + [VMEM] * 9,
+        out_specs=(VMEM,) * 3,
+        compiler_params=pltpu.CompilerParams(vmem_limit_bytes=48 << 20),
+        name="attend_back",
+    )(half, *arrays)
+
+
+def swap_fsdp(value):
+    return lax.ppermute(value, "fsdp", [(0, 1), (1, 0)])
+
+
+def swap_half(value):
+    return lax.ppermute(value, "seq", [(i, i ^ SQUARE) for i in range(SEQ)])
+
+
+def in_order(flag, mine, other, axis):
+    return jnp.where(
+        flag == 0, jnp.stack([mine, other], axis=axis), jnp.stack([other, mine], axis=axis)
+    )
+
+
+def four_parts(half, fsdp, block, axis):
+    across = swap_half(block)
+    near = in_order(fsdp, block, swap_fsdp(block), axis)
+    far = in_order(fsdp, across, swap_fsdp(across), axis)
+    return in_order(half, near, far, 0)
+
+
+def keep_part(value, index, axis):
+    mine = lax.dynamic_index_in_dim(value, index, axis, keepdims=False)
+    other = lax.dynamic_index_in_dim(value, 1 - index, axis, keepdims=False)
+    return mine, other
+
+
+def sum_fsdp(value, fsdp, axis):
+    mine, other = keep_part(value, fsdp, axis)
+    return mine + swap_fsdp(other.astype(LOW)).astype(jnp.float32)
+
+
+def sum_half(value, half):
+    mine, other = keep_part(value, half, 0)
+    return mine + swap_half(other.astype(LOW)).astype(jnp.float32)
+
+
+def turn(values_t, cosine, sine):
+    former, latter = values_t[:, : HEAD_DIM // 2], values_t[:, HEAD_DIM // 2 :]
+    return jnp.concatenate(
+        [former * cosine - latter * sine, latter * cosine + former * sine], axis=1
+    )
+
+
+def local_squares(
+    tokens,
+    cotangent,
+    lengths,
+    mix_weight,
+    out_weight,
+    in_weight,
+    down_weight,
+    norm_gains,
+    mix_first,
+    out_first,
+    in_first,
+    down_first,
+    norm_first,
+    mix_second,
+    out_second,
+    in_second,
+    down_second,
+    norm_second,
+):
+    f32 = jnp.float32
+    fsdp = lax.axis_index("fsdp")
+    seq = lax.axis_index("seq")
+    half, member = seq // SQUARE, seq % SQUARE
+    doc_lens = lax.dynamic_index_in_dim(lengths, fsdp, 0, keepdims=False)
+    places = half * KEYS + jnp.arange(KEYS, dtype=jnp.int32)
+    segment, positions = doc_layout(places, doc_lens)
+    other_segment, _ = doc_layout(jnp.arange(KEYS, dtype=jnp.int32), doc_lens)
+    keep_t = (segment < doc_lens.shape[0]).astype(f32)[None, :]
+    inverse = ROPE_BASE ** (-jnp.arange(HEAD_DIM // 2, dtype=f32) * 2.0 / HEAD_DIM)
+    angles = inverse[:, None] * positions.astype(f32)[None, :]
+    cosine, sine = jnp.cos(angles), jnp.sin(angles)
+
+    wide = 2 * HEAD_DIM
+    key_width = KV_HEADS * HEAD_DIM
+    mix_low = mix_weight[0].astype(LOW)
+    share = mix_low.shape[0]
+    mix_blocks = jnp.concatenate(
+        [
+            mix_low[:, :D].reshape(share, SQUARE, wide),
+            mix_low[:, D : D + key_width].reshape(share, SQUARE, HEAD_DIM),
+            mix_low[:, D + key_width :].reshape(share, SQUARE, HEAD_DIM),
+        ],
+        axis=2,
+    ).transpose(1, 0, 2)
+    unit = FF // FLEET
+    in_blocks = (
+        in_weight[0]
+        .astype(LOW)
+        .reshape(share, 2, 2, SQUARE, 2 * unit)
+        .transpose(3, 0, 1, 2, 4)
+        .reshape(SQUARE, share, 8 * unit)
+    )
+    out_low = out_weight[0].astype(LOW)
+    down_low = down_weight[0].astype(LOW)
+    gain_block = jnp.pad(norm_gains[0].astype(LOW), ((0, 14), (0, 128 - share)))
+    tok_all, cot_all, gain_all, mix_full, in_square, out_mine = first_exchange(
+        tokens, cotangent, gain_block, mix_blocks, in_blocks, out_low
+    )
+    rows = SQUARE * ROWS
+    tok_all = tok_all.reshape(rows, D)
+    cot_all = cot_all.reshape(rows, D)
+    gains = gain_all[:, :2, :share].transpose(1, 0, 2).reshape(2, D).astype(f32)
+    gain_attn, gain_mlp = gains[0], gains[1]
+    mix_full = mix_full.reshape(D, 4 * HEAD_DIM)
+    out_mine = out_mine.reshape(wide, D)
+    in_mine = four_parts(half, fsdp, in_square, 1).reshape(D, 8 * unit)
+    down_mine = four_parts(half, fsdp, down_low, 0).reshape(4 * unit, D)
+
+    normed_low = normalize(tok_all.astype(f32), gain_attn)[0].astype(LOW)
+    projected_t = dot32(mix_full, normed_low, ((0,), (1,)))
+    heads_t = turn(projected_t[: 3 * HEAD_DIM].reshape(3, HEAD_DIM, rows), cosine, sine).astype(LOW)
+    value_t = projected_t[3 * HEAD_DIM :].astype(LOW)
+    kinds = jnp.arange(6, dtype=jnp.int32)
+    query_t = jnp.concatenate(
+        [
+            heads_t[:2],
+            jnp.broadcast_to(
+                (segment[None, :] == kinds[:, None]).astype(LOW)[None], (2, 6, rows)
+            ),
+            jnp.zeros((2, 26, rows), LOW),
+        ],
+        axis=1,
+    )
+    key_value_t = jnp.concatenate([heads_t[2], value_t], axis=0)
+    arrived_t = lax.ppermute(key_value_t, "seq", [(i, i + SQUARE) for i in range(SQUARE)])
+    both_t = jnp.concatenate([arrived_t, key_value_t], axis=1)
+    keys_t, values_t = both_t[:HEAD_DIM], both_t[HEAD_DIM:]
+    all_segment = jnp.concatenate([other_segment, segment])
+    keys_r = jnp.concatenate(
+        [
+            keys_t.T,
+            jnp.where(all_segment[:, None] == kinds[None, :], 0.0, -WALL).astype(LOW),
+            jnp.zeros((2 * rows, 26), LOW),
+        ],
+        axis=1,
+    )
+    half_flag = half.astype(jnp.int32).reshape(1)
+    mixed_t, log_sum = attend(half_flag, query_t, keys_r, values_t)
+    attended_t = mixed_t.reshape(wide, rows) * keep_t
+    attended_low = attended_t.astype(LOW)
+    out_part = dot32(attended_low, out_mine, ((0,), (0,))).astype(LOW)
+    stream = tokens.astype(f32)
+    middle = stream + square_scatter(out_part)
+
+    normed_two, unit_mlp, scale_mlp = normalize(middle, gain_mlp)
+    two_all = square_gather(normed_two.astype(LOW))
+    gate_up = dot32(two_all, in_mine)
+    gate, up = gate_up[:, : 4 * unit], gate_up[:, 4 * unit :]
+    sigmoid_gate = jax.nn.sigmoid(gate)
+    hidden_low = (gate * sigmoid_gate * up).astype(LOW)
+    y_part = dot32(hidden_low, down_mine).astype(LOW)
+    grad_hidden = dot32(cot_all, down_mine, ((1,), (1,)))
+    grad_gate = grad_hidden * up * sigmoid_gate * (1.0 + gate * (1.0 - sigmoid_gate))
+    grad_up = grad_hidden * gate * sigmoid_gate
+    grad_gate_up = jnp.concatenate([grad_gate, grad_up], axis=1).astype(LOW)
+    two_part = dot32(grad_gate_up, in_mine, ((1,), (1,))).astype(LOW)
+    grad_normed_two = square_scatter(two_part)
+    grad_down = dot32(hidden_low, cot_all, ((0,), (0,)))
+    grad_in = dot32(two_all, grad_gate_up, ((0,), (0,)))
+    grad_stream = cotangent.astype(f32)
+    grad_gain_mlp, grad_middle_norm = norm_backward(grad_normed_two, unit_mlp, scale_mlp, gain_mlp)
+    grad_middle = grad_stream + grad_middle_norm
+    hidden_out = (middle + square_scatter(y_part)).astype(LOW)
+    in_sum = sum_half(sum_fsdp(grad_in.reshape(2, SQUARE, 2, share, 8 * unit), fsdp, 2), half)
+    down_sum = sum_half(sum_fsdp(grad_down.reshape(2, 2, unit, D), fsdp, 1), half)
+
+    branch_all = square_gather(grad_middle.astype(LOW))
+    grad_out = dot32(attended_low, branch_all)
+    out_sum = sum_fsdp(grad_out.reshape(2, 2, share, D), fsdp, 1)
+    grad_att = dot32(out_mine, branch_all, ((1,), (1,))) * keep_t
+    grad_t = grad_att.astype(LOW).reshape(2, HEAD_DIM, rows)
+    delta = jnp.sum(
+        grad_t.astype(f32) * attended_t.reshape(2, HEAD_DIM, rows), axis=1
+    )
+    dq_t, dk, dv = attend_back(
+        half_flag,
+        query_t,
+        heads_t[:2].transpose(0, 2, 1),
+        keys_r,
+        keys_t,
+        values_t.T,
+        grad_t,
+        grad_t.transpose(0, 2, 1),
+        log_sum,
+        delta,
+    )
+    pair = jnp.concatenate([dk, dv], axis=1)
+    returned = lax.ppermute(
+        pair[:KEYS].astype(LOW), "seq", [(i + SQUARE, i) for i in range(SQUARE)]
+    )
+    pair_t = (pair[KEYS:] + returned.astype(f32)).T
+    scale = HEAD_DIM ** (-0.5)
+    turned = turn(
+        jnp.concatenate([dq_t, pair_t[None, :HEAD_DIM]], axis=0) * scale, cosine, -sine
+    )
+    grad_projected_t = jnp.concatenate(
+        [turned.reshape(3 * HEAD_DIM, rows), pair_t[HEAD_DIM:]], axis=0
+    ).astype(LOW)
+    grad_mix = dot32(normed_low, grad_projected_t, ((0,), (1,)))
+    mix_sum = sum_half(sum_fsdp(grad_mix.reshape(2, SQUARE, 2, share, 4 * HEAD_DIM), fsdp, 2), half)
+    normed_part = dot32(grad_projected_t, mix_full, ((0,), (1,))).astype(LOW)
+    grad_normed = square_scatter(normed_part)
+    _, unit_attn, scale_attn = normalize(stream, gain_attn)
+    grad_gain_attn, grad_input_norm = norm_backward(grad_normed, unit_attn, scale_attn, gain_attn)
+    grad_tokens = grad_middle + grad_input_norm
+
+    gain_blocks = jnp.pad(
+        jnp.stack([grad_gain_attn, grad_gain_mlp]).reshape(2, FLEET, share).transpose(1, 0, 2),
+        ((0, 0), (0, 6), (0, 128 - share)),
+    )
+    in_got, mix_got, out_got, gain_got = last_exchange(
+        in_sum.astype(LOW), mix_sum.astype(LOW), out_sum.astype(LOW), gain_blocks
+    )
+    in_grad = (
+        in_got.reshape(SQUARE, share, 2, 2, 2 * unit)
+        .transpose(1, 2, 3, 0, 4)
+        .reshape(1, share, 2 * FF)
+        .astype(f32)
+    )
+    mix_got = mix_got.transpose(1, 0, 2)
+    mix_grad = jnp.concatenate(
+        [
+            mix_got[:, :, :wide].reshape(share, D),
+            mix_got[:, :, wide : wide + HEAD_DIM].reshape(share, key_width),
+            mix_got[:, :, wide + HEAD_DIM :].reshape(share, key_width),
+        ],
+        axis=1,
+    ).astype(f32)[None]
+    out_grad = jnp.sum(out_got.astype(f32), axis=0)[None]
+    down_grad = down_sum[None]
+    norm_grad = jnp.sum(gain_got[:, :2, :share], axis=0)[None]
+    squares = sum(
+        jnp.sum(grad * grad) for grad in (mix_grad, out_grad, in_grad, down_grad, norm_grad)
+    )
+    total_squares = jnp.sum(share_all(jnp.broadcast_to(squares, (8, 128)))[:, 0, 0])
+    grad_norm = jnp.sqrt(total_squares)
+    clip_scale = CLIP_NORM / jnp.maximum(grad_norm, CLIP_NORM)
+    results = [hidden_out, grad_tokens, grad_norm]
+    for weight, first, second, grad, rate in (
+        (mix_weight, mix_first, mix_second, mix_grad, LEARN_RATE),
+        (out_weight, out_first, out_second, out_grad, OUT_RATE),
+        (in_weight, in_first, in_second, in_grad, LEARN_RATE),
+        (down_weight, down_first, down_second, down_grad, LEARN_RATE),
+        (norm_gains, norm_first, norm_second, norm_grad, GAIN_RATE),
+    ):
+        new, moment, square = adam_update(weight, first, second, grad, clip_scale, rate)
+        results += [grad, new, moment, square, new.astype(LOW)]
+    return tuple(results)
+
+
 def solution(mesh):
+    squares = mesh.shape["seq"] == SEQ and mesh.shape["fsdp"] == 2
     return jax.shard_map(
-        local,
+        local_squares if squares else local,
         mesh=mesh,
         in_specs=(
             P(("seq", "fsdp"), None),

time: 2010 us -> 561 us (0.28)
  waiting for transfers between devices: 1530 us -> 98.1 us
  Pallas kernels: 0 us -> 250 us
  matrix products: 170 us -> 39.6 us
  blocking collectives: 117 us -> 0 us
  starting transfers between devices: 1.43 us -> 24.6 us
    reduce_scatter x5 -> x0, waiting for transfers between devices: 1100 us -> none  [the longest x1 434 us: layer_backward(): lax.psum_scatter(grad_in, ('seq', 'fsdp'), scatter_dimension=0, tiled=True)]
    all_gather x6 -> x0, waiting for transfers between devices: 333 us -> none  [the longest x1 153 us: fetch_layer(): lax.all_gather(in_weight[layer_index].astype(jnp.bfloat16), ('seq', 'fsdp...]
    pallas_call x0 -> x11, Pallas kernels: none -> 250 us  [the longest x4 90 us: square_scatter(): pl.pallas_call(scatter_kernel, out_shape=jax.ShapeDtypeStruct((ROWS, widt...]
    dot_general x40 -> x12, matrix products: 170 us -> 39.6 us  [dot32(): lax.dot_general(left, right, (dims, ((), ())), preferred_element_type=jnp...]
    unnamed x13 -> x0, waiting for transfers between devices: 99.5 us -> none
    ppermute x0 -> x15, waiting for transfers between devices: none -> 98.1 us  [the longest x5 56.9 us: swap_half(): return lax.ppermute(value, 'seq', [(i, i ^ SQUARE) for i in range(SEQ)])]
    all_gather x1 -> x0, blocking collectives: 78 us -> none  [fetch_layer(): lax.all_gather(norm_gains[layer_index].astype(jnp.bfloat16), ('seq', 'fsd...]
    psum x1 -> x0, blocking collectives: 39 us -> none  [local(): total_squares = lax.psum(squares, ('seq', 'fsdp'))]
  transfers between devices with their start and end apart: 12 -> 15, of which waited for: 11 -> 4; matrix products, arithmetic and copies ran while one was open for 9% -> 16% of each run, Pallas kernels for 0% -> 36%
where the time goes in v1:
time: 561 us; the launch traced here: 552 us
  Pallas kernels  250 us (45%)
  waiting for transfers between devices  98.1 us (17%)
  other arithmetic  76 us (14%)
  local copies, waits for them, and re-layouts  55.9 us (10%)
  matrix products  39.6 us (7%)
  starting transfers between devices  24.6 us (4%)
  between operations  7.63 us (1%)
    pallas_call x4, Pallas kernels, square_scatter(): pl.pallas_call(scatter_kernel, out_shape=jax.ShapeDtypeStruct((ROWS, widt...  90 us
    pallas_call x1, Pallas kernels, first_exchange(): pl.pallas_call(first_kernel, out_shape=(shape((SQUARE,) + tok.shape, LOW)...  78.4 us
    ppermute x5, waiting for transfers between devices, swap_half(): return lax.ppermute(value, 'seq', [(i, i ^ SQUARE) for i in range(SEQ)])  56.9 us
    ppermute x1, waiting for transfers between devices, local_squares(): lax.ppermute(pair[:KEYS].astype(LOW), 'seq', [(i + SQUARE, i) for i in ra...  40.1 us
    dot_general x12, matrix products, dot32(): lax.dot_general(left, right, (dims, ((), ())), preferred_element_type=jnp...  39.6 us
    pallas_call x2, Pallas kernels, square_gather(): pl.pallas_call(gather_kernel, out_shape=jax.ShapeDtypeStruct((SQUARE,) +...  35.3 us
    pallas_call x1, Pallas kernels, last_exchange(): pl.pallas_call(last_kernel, out_shape=tuple((shape(v.shape, v.dtype) for...  25.4 us
    unnamed x160, local copies, waits for them, and re-layouts  15.8 us
  transfers between devices with their start and end apart: 15, of which 4 were waited for; matrix products, arithmetic and copies ran while one was open for 16% of the time, Pallas kernels for 36%

profile of v1, /device:TPU:0, one launch (start us, length us, event | category | flops | bytes accessed | tf_op | source)
XLA Modules:
  0.0 551.9 jit_solution(15244824178257853760)
XLA Ops:
  0.7 2.1 convert_bitcast_fusion.2
  2.8 4.0 collective-permute-start.5
  6.9 1.5 collective-permute-start.4
  10.6 1.4 reshape.880.inn
  13.5 78.4 %first_exchange.1 = (bf16[8,128,1536]{2,1,0:T(8,128)(2,1)}, bf16[8,128,1536]{2,1,0:T(8,128)(2,1)}, bf16[32,16,128]{2,1,0:T(8,128)(2,1)}, bf16[32,48,384]{2,1,0:T...) custom-call(bf16[128,1536]{1,0:T(8,128)(2,1)} %tok.1, bf16[128,1536]{1,0:T(8,128)(2,1)} %cot.1, ...), custom_call_target="tpu_custom_call" | custom-call | tf_op jit(solution)/shard_map/first_exchange/pallas_call | solution.py:658
  92.0 2.7 collective-permute-start.1
  94.7 2.7 multiply_reduce_fusion
  99.7 1.4 fusion.64
  103.4 1.5 copy.121
  105.0 1.6 copy.122
  106.6 2.9 fusion.38
  111.5 5.8 %collective-permute-start = (bf16[192,1024]{0,1:T(8,128)(2,1)}, bf16[192,1024]{0,1:T(8,128)(2,1)}, u32[]{:S(2)}, u32[]{:S(2)}) collective-permute-start(bf16[192,1024]{0,1:T(8,128)(2,1)} %pad_maximum_fusion.6), channel_id=1, source_target_pairs={{0,16},{2,18},{4,20},{6,22},{8,24},{10,26},{12,28},{14,30},{1,17},... | collective-permute-start | bytes 1179656 | tf_op jit(solution)/shard_map/ppermute | solution.py:1132
  118.5 4.4 fusion.1
  123.0 4.6 copy.109
  131.8 4.7 attend.1
  137.7 37.8 %square_scatter.4 = f32[128,1536]{1,0:T(8,128)S(1)} custom-call(bf16[8,128,1536]{2,1,0:T(8,128)(2,1)S(1)} %bitcast.191), custom_call_target="tpu_custom_call" | custom-call | tf_op jit(solution)/shard_map/square_scatter/pallas_call | solution.py:769
  177.1 1.8 collective-permute-start.6
  179.0 2.0 multiply_convert_fusion.4.src
  182.4 2.0 copy.102.keys_t
  184.4 18.1 %square_gather.2 = bf16[8,128,1536]{2,1,0:T(8,128)(2,1)} custom-call(bf16[128,1536]{1,0:T(8,128)(2,1)} %multiply_convert_fusion.4.src), custom_call_target="tpu_custom_call" | custom-call | tf_op jit(solution)/shard_map/square_gather/pallas_call | solution.py:693
  202.5 4.7 copy.106
  207.2 2.2 maximum_select_fusion.1
  210.9 2.7 maximum_select_fusion.2
  214.5 1.6 copy-done.10
  216.0 3.6 fusion.65
  219.6 3.5 multiply_convert_fusion.2
  223.2 12.4 %convolution_convert_fusion.3 = bf16[1024,1536]{1,0:T(8,128)(2,1)S(1)} fusion(bf16[1536,1024]{1,0:T(8,128)(2,1)S(1)} %bitcast.212, bf16[1024,512]{0,1:T(8,128)(2,1)S(1)} %get-tuple-element.92, bf16[1024,512]{0,1:T(8,128)(2,1)S(1)} %get-tuple-element.91), kind=kOutput, calls=%fused_computation.8 | convolution fusion | flops 3226992640 | bytes 8388608 | tf_op jit(solution)/shard_map/dot_general | solution.py:889
  235.6 17.7 %square_scatter.6 = f32[128,1536]{1,0:T(8,128)S(1)} custom-call(bf16[8,128,1536]{2,1,0:T(8,128)(2,1)S(1)} %bitcast.198), custom_call_target="tpu_custom_call" | custom-call | tf_op jit(solution)/shard_map/square_scatter/pallas_call | solution.py:769
  253.4 2.1 multiply_reduce_fusion.3
  257.4 2.3 fusion.50.src
  259.6 3.2 convolution_convert_fusion.2
  262.9 1.8 fusion.67
  266.8 3.5 fusion.2
  270.3 1.6 fusion.5
  271.9 1.6 copy-done.24
  273.5 17.1 %square_scatter.5 = f32[128,1536]{1,0:T(8,128)S(1)} custom-call(bf16[8,128,1536]{2,1,0:T(8,128)(2,1)S(1)} %bitcast.196), custom_call_target="tpu_custom_call" | custom-call | tf_op jit(solution)/shard_map/square_scatter/pallas_call | solution.py:769
  292.6 17.3 %square_gather.3 = bf16[8,128,1536]{2,1,0:T(8,128)(2,1)} custom-call(bf16[128,1536]{1,0:T(8,128)(2,1)} %fusion.50.src), custom_call_target="tpu_custom_call" | custom-call | tf_op jit(solution)/shard_map/square_gather/pallas_call | solution.py:693
  309.9 2.8 fusion.66
  321.6 6.7 %attend_back.1 = (f32[2,96,1024]{2,1,0:T(8,128)S(1)}, f32[2048,96]{1,0:T(8,128)S(1)}, f32[2048,96]{1,0:T(8,128)}) custom-call(s32[1]{0:T(128)} %bitcast.half, bf16[2,128,1024]{2,1,0:T(8,128)(2,1)S(1)} %copy.97.query_t, bf16[2,1024,96]{2,1,0:T(8,128)(2,1)S(1)} %bitcast.192, bf16[2048,128]{1,0:T(8,128)(2,1)S(1)} %maximum_maximum_fusion.2.keys, ...), custom_call_target="tpu_custom_call" | custom-call | tf_op jit(solution)/shard_map/attend_back/pallas_call | solution.py:989
  329.2 1.5 copy.103
  334.5 1.7 fusion.29.out
  336.3 40.1 %collective-permute-done.7 = bf16[1024,192]{1,0:T(8,128)(2,1)S(1)} collective-permute-done((bf16[1024,192]{1,0:T(8,128)(2,1)S(1)}, bf16[1024,192]{1,0:T(8,128)(2,1)S(1)}, u32[]{:S(2)}, u32[]{:S(2)}) %collective-permute-start.7) | collective-permute-done | bytes 393248 | tf_op jit(solution)/shard_map/ppermute | solution.py:1195
  379.5 3.3 convolution_convert_fusion.1
  382.8 1.8 fusion.25
  386.7 17.3 %square_scatter.7 = f32[128,1536]{1,0:T(8,128)S(1)} custom-call(bf16[8,128,1536]{2,1,0:T(8,128)(2,1)S(1)} %bitcast.197), custom_call_target="tpu_custom_call" | custom-call | tf_op jit(solution)/shard_map/square_scatter/pallas_call | solution.py:769
  405.2 2.6 fusion.18
  409.3 3.1 bitcast_add_fusion
  412.5 3.0 collective-permute-start.9
  417.6 35.9 %collective-permute-done.14 = bf16[128,1536]{1,0:T(8,128)(2,1)S(1)} collective-permute-done((bf16[128,1536]{1,0:T(8,128)(2,1)S(1)}, bf16[128,1536]{1,0:T(8,128)(2,1)S(1)}, u32[]{:S(2)}, u32[]{:S(2)}) %collective-permute-start.14) | collective-permute-done | bytes 393248 | tf_op jit(solution)/shard_map/ppermute | solution.py:1008
  453.4 1.6 fusion.49
  455.1 21.0 %collective-permute-done.11 = bf16[8,48,384]{2,1,0:T(8,128)(2,1)S(1)} collective-permute-done((bf16[8,48,384]{2,1,0:T(8,128)(2,1)S(1)}, bf16[8,48,384]{2,1,0:T(8,128)(2,1)S(1)}, u32[]{:S(2)}, u32[]{:S(2)}) %collective-permute-start.11) | collective-permute-done | bytes 294944 | tf_op jit(solution)/shard_map/ppermute | solution.py:1008
  478.1 25.4 %last_exchange.1 = (bf16[8,48,1024]{2,1,0:T(8,128)(2,1)}, bf16[8,48,384]{2,1,0:T(8,128)(2,1)}, bf16[2,48,1536]{2,1,0:T(8,128)(2,1)}, f32[32,8,128]{2,1,0:T(8,128)}) custom-call(bf16[8,48,1024]{2,1,0:T(8,128)(2,1)} %fusion.6.inn, bf16[8,48,384]{2,1,0:T(8,128)(2,1)} %fusion.30.mix, bf16[2,48,1536]{2,1,0:T(8,128)(2,1)} %fusion.29.out, f32[32,8,128]{2,1,0:T(8,128)} %pad.9.gain), custom_call_target="tpu_custom_call" | custom-call | tf_op jit(solution)/shard_map/last_exchange/pallas_call | solution.py:847
  504.4 1.7 fusion.62
  506.1 2.1 multiply_reduce_fusion.1
  508.3 2.6 reshape.897
  516.8 2.4 multiply_reduce_fusion.7
  523.1 9.6 %share_all.1 = f32[32,8,128]{2,1,0:T(8,128)} custom-call(f32[8,128]{1,0:T(8,128)} %broadcast_in_dim.30.value), custom_call_target="tpu_custom_call" | custom-call | tf_op jit(solution)/shard_map/share_all/pallas_call | solution.py:877
  532.8 1.5 slice_reduce_fusion.3
  535.0 2.1 copy.115
  537.1 1.6 reshape.896
  539.4 2.7 fusion.57
  542.1 2.8 fusion.59
  545.1 3.3 fusion.55
  548.4 2.0 fusion.53
  (275 shorter events, 61.5 us)
Async XLA Ops:
  0.7 7.7 %copy-start.31 = (f32[1,48,3072]{2,1,0:T(8,128)S(1)}, f32[1,48,3072]{2,1,0:T(8,128)}, u32[]{:S(2)}) copy-start(f32[1,48,3072]{2,1,0:T(8,128)} %param.21) | copy-start | bytes 1769476
  0.7 7.8 %copy-start.65 = (f32[1,2,48]{2,1,0:T(2,128)S(1)}, f32[1,2,48]{2,1,0:T(2,128)}, u32[]{:S(2)}) copy-start(f32[1,2,48]{2,1,0:T(2,128)} %param.25) | copy-start | bytes 1156
  0.7 7.8 %copy-start.47 = (f32[1,48,1536]{2,1,0:T(8,128)S(1)}, f32[1,48,1536]{2,1,0:T(8,128)}, u32[]{:S(2)}) copy-start(f32[1,48,1536]{2,1,0:T(8,128)} %param.22) | copy-start | bytes 884740
  2.8 6.9 %copy-start.14 = (f32[1,48,8192]{2,1,0:T(8,128)S(1)}, f32[1,48,8192]{2,1,0:T(8,128)}, u32[]{:S(2)}) copy-start(f32[1,48,8192]{2,1,0:T(8,128)} %param.23) | copy-start | bytes 4718596
  2.8 174.3 %collective-permute-start.5 = (bf16[128,1536]{1,0:T(8,128)(2,1)}, bf16[128,1536]{1,0:T(8,128)(2,1)}, u32[]{:S(2)}, u32[]{:S(2)}) collective-permute-start(bf16[128,1536]{1,0:T(8,128)(2,1)} %get-tuple-element.109), channel_id=1, source_target_pairs={{0,16},{2,18},{4,20},{6,22},{8,24},{10,26},{12,28},{14,30},{16,0},... | collective-permute-start | bytes 1179656 | tf_op jit(solution)/shard_map/ppermute | solution.py:1008
  6.9 174.3 %collective-permute-start.4 = (bf16[128,1536]{1,0:T(8,128)(2,1)}, bf16[128,1536]{1,0:T(8,128)(2,1)}, u32[]{:S(2)}, u32[]{:S(2)}) collective-permute-start(bf16[128,1536]{1,0:T(8,128)(2,1)} %get-tuple-element.109), channel_id=1, source_target_pairs={{0,1},{1,0},{2,3},{3,2},{4,5},{5,4},{6,7},{7,6},{8,9},{9,8},{10,11... | collective-permute-start | bytes 1179656 | tf_op jit(solution)/shard_map/ppermute | solution.py:1004
  91.9 89.1 %collective-permute-start.2 = (bf16[8,48,1024]{2,1,0:T(8,128)(2,1)}, bf16[8,48,1024]{2,1,0:T(8,128)(2,1)}, u32[]{:S(2)}, u32[]{:S(2)}) collective-permute-start(bf16[8,48,1024]{2,1,0:T(8,128)(2,1)} %get-tuple-element.48), channel_id=1, source_target_pairs={{0,16},{2,18},{4,20},{6,22},{8,24},{10,26},{12,28},{14,30},{16,0},... | collective-permute-start | bytes 2359304 | tf_op jit(solution)/shard_map/ppermute | solution.py:1008
  92.0 115.2 %collective-permute-start.1 = (bf16[8,48,1024]{2,1,0:T(8,128)(2,1)}, bf16[8,48,1024]{2,1,0:T(8,128)(2,1)}, u32[]{:S(2)}, u32[]{:S(2)}) collective-permute-start(bf16[8,48,1024]{2,1,0:T(8,128)(2,1)} %get-tuple-element.48), channel_id=1, source_target_pairs={{0,1},{1,0},{2,3},{3,2},{4,5},{5,4},{6,7},{7,6},{8,9},{9,8},{10,11... | collective-permute-start | bytes 2359304 | tf_op jit(solution)/shard_map/ppermute | solution.py:1004
  94.7 3.8 copy-start.8
  111.5 17.1 %collective-permute-start = (bf16[192,1024]{0,1:T(8,128)(2,1)}, bf16[192,1024]{0,1:T(8,128)(2,1)}, u32[]{:S(2)}, u32[]{:S(2)}) collective-permute-start(bf16[192,1024]{0,1:T(8,128)(2,1)} %pad_maximum_fusion.6), channel_id=1, source_target_pairs={{0,16},{2,18},{4,20},{6,22},{8,24},{10,26},{12,28},{14,30},{1,17},... | collective-permute-start | bytes 1179656 | tf_op jit(solution)/shard_map/ppermute | solution.py:1132
  118.5 60.4 %copy-start.53 = (f32[1536]{0:T(1024)}, f32[1536]{0:T(1024)S(1)}, u32[]{:S(2)}) copy-start(f32[1536]{0:T(1024)S(1)} %mul.670) | copy-start | bytes 18436
  131.5 5.1 copy-start.57
  131.8 4.8 copy-start.51
  137.7 37.8 %copy-start.11 = (bf16[128,1536]{1,0:T(8,128)(2,1)S(1)}, bf16[128,1536]{1,0:T(8,128)(2,1)}, u32[]{:S(2)}) copy-start(bf16[128,1536]{1,0:T(8,128)(2,1)} %tok.1) | copy-start | bytes 1179652
  175.5 5.6 %copy-start.40 = (bf16[1,1,128,1536]{3,2,1,0:T(8,128)(2,1)S(1)}, bf16[1,1,128,1536]{3,2,1,0:T(8,128)(2,1)}, u32[]{:S(2)}) copy-start(bf16[1,1,128,1536]{3,2,1,0:T(8,128)(2,1)} %get-tuple-element.108) | copy-start | bytes 1179652
  177.1 4.1 copy-start.59
  177.1 32.3 %collective-permute-start.6 = (bf16[128,1536]{1,0:T(8,128)(2,1)}, bf16[128,1536]{1,0:T(8,128)(2,1)S(1)}, u32[]{:S(2)}, u32[]{:S(2)}) collective-permute-start(bf16[128,1536]{1,0:T(8,128)(2,1)} %collective-permute-done.5), channel_id=1, source_target_pairs={{0,1},{1,0},{2,3},{3,2},{4,5},{5,4},{6,7},{7,6},{8,9},{9,8},{10,11... | collective-permute-start | bytes 1179656 | tf_op jit(solution)/shard_map/ppermute | solution.py:1004
  181.0 29.9 %collective-permute-start.3 = (bf16[8,48,1024]{2,1,0:T(8,128)(2,1)}, bf16[8,48,1024]{2,1,0:T(8,128)(2,1)}, u32[]{:S(2)}, u32[]{:S(2)}) collective-permute-start(bf16[8,48,1024]{2,1,0:T(8,128)(2,1)} %collective-permute-done.2), channel_id=1, source_target_pairs={{0,1},{1,0},{2,3},{3,2},{4,5},{5,4},{6,7},{7,6},{8,9},{9,8},{10,11... | collective-permute-start | bytes 2359304 | tf_op jit(solution)/shard_map/ppermute | solution.py:1004
  210.9 8.7 %copy-start.38 = (bf16[2,2,128,1536]{3,2,1,0:T(8,128)(2,1)}, bf16[2,2,128,1536]{3,2,1,0:T(8,128)(2,1)S(1)}, u32[]{:S(2)}) copy-start(bf16[2,2,128,1536]{3,2,1,0:T(8,128)(2,1)S(1)} %maximum_select_fusion.3) | copy-start | bytes 4718596
  216.0 3.6 copy-start.70
  223.2 12.4 %copy-start.74 = (bf16[1024,512]{0,1:T(8,128)(2,1)}, bf16[1024,512]{0,1:T(8,128)(2,1)S(1)}, u32[]{:S(2)}) copy-start(bf16[1024,512]{0,1:T(8,128)(2,1)S(1)} %get-tuple-element.91) | copy-start | bytes 3145732
  223.2 12.4 %copy-start.76 = (bf16[1024,512]{0,1:T(8,128)(2,1)}, bf16[1024,512]{0,1:T(8,128)(2,1)S(1)}, u32[]{:S(2)}) copy-start(bf16[1024,512]{0,1:T(8,128)(2,1)S(1)} %get-tuple-element.92) | copy-start | bytes 3145732
  235.6 17.8 %copy-start.54 = (f32[1536]{0:T(1024)S(1)}, f32[1536]{0:T(1024)}, u32[]{:S(2)}) copy-start(f32[1536]{0:T(1024)} %copy-done.53) | copy-start | bytes 18436
  235.6 17.8 %copy-start.60 = (f32[128]{0:T(128)S(1)}, f32[128]{0:T(128)}, u32[]{:S(2)}) copy-start(f32[128]{0:T(128)} %copy-done.59) | copy-start | bytes 1540
  253.4 4.0 copy-start.25
  259.6 3.2 copy-start.71
  259.6 3.3 copy-start.73
  262.9 3.9 copy-start.28
  262.9 3.9 copy-start.77
  265.7 142.1 %collective-permute-start.13 = (bf16[2,128,1536]{2,1,0:T(8,128)(2,1)}, bf16[2,128,1536]{2,1,0:T(8,128)(2,1)}, u32[]{:S(2)}, u32[]{:S(2)}) collective-permute-start(bf16[2,128,1536]{2,1,0:T(8,128)(2,1)} %fusion.24), channel_id=1, source_target_pairs={{0,1},{1,0},{2,3},{3,2},{4,5},{5,4},{6,7},{7,6},{8,9},{9,8},{10,11... | collective-permute-start | bytes 2359304 | tf_op jit(solution)/shard_map/ppermute | solution.py:1004
  291.5 18.4 %copy-start.18 = (bf16[2,96,1024]{2,1,0:T(8,128)(2,1)S(1)}, bf16[2,96,1024]{2,1,0:T(8,128)(2,1)}, u32[]{:S(2)}) copy-start(bf16[2,96,1024]{2,1,0:T(8,128)(2,1)} %copy-done.17) | copy-start | bytes 1179652
  291.5 117.8 %collective-permute-start.8 = (bf16[2,8,48,1024]{3,2,1,0:T(8,128)(2,1)}, bf16[2,8,48,1024]{3,2,1,0:T(8,128)(2,1)}, u32[]{:S(2)}, u32[]{:S(2)}) collective-permute-start(bf16[2,8,48,1024]{3,2,1,0:T(8,128)(2,1)} %fusion.5), channel_id=1, source_target_pairs={{0,1},{1,0},{2,3},{3,2},{4,5},{5,4},{6,7},{7,6},{8,9},{9,8},{10,11... | collective-permute-start | bytes 4718600 | tf_op jit(solution)/shard_map/ppermute | solution.py:1004
  309.9 4.6 copy-start.9
  309.9 4.6 copy-start.52
  309.9 4.6 copy-start.58
  313.6 21.0 %collective-permute-start.12 = (bf16[2,48,1536]{2,1,0:T(8,128)(2,1)}, bf16[2,48,1536]{2,1,0:T(8,128)(2,1)}, u32[]{:S(2)}, u32[]{:S(2)}) collective-permute-start(bf16[2,48,1536]{2,1,0:T(8,128)(2,1)} %fusion.36), channel_id=1, source_target_pairs={{0,1},{1,0},{2,3},{3,2},{4,5},{5,4},{6,7},{7,6},{8,9},{9,8},{10,11... | collective-permute-start | bytes 884744 | tf_op jit(solution)/shard_map/ppermute | solution.py:1004
  330.7 3.8 copy-start.23
  330.7 45.6 %copy-start.21 = (f32[2048,96]{1,0:T(8,128)S(1)}, f32[2048,96]{1,0:T(8,128)}, u32[]{:S(2)}) copy-start(f32[2048,96]{1,0:T(8,128)} %get-tuple-element.53) | copy-start | bytes 2359300
  332.1 44.2 %collective-permute-start.7 = (bf16[1024,192]{1,0:T(8,128)(2,1)S(1)}, bf16[1024,192]{1,0:T(8,128)(2,1)S(1)}, u32[]{:S(2)}, u32[]{:S(2)}) collective-permute-start(bf16[1024,192]{1,0:T(8,128)(2,1)S(1)} %fusion.14), channel_id=1, source_target_pairs={{16,0},{18,2},{20,4},{22,6},{24,8},{26,10},{28,12},{30,14},{17,1},... | collective-permute-start | bytes 1179656 | tf_op jit(solution)/shard_map/ppermute | solution.py:1195
  379.5 3.3 copy-start.27
  385.7 29.8 %collective-permute-start.10 = (bf16[2,8,48,384]{3,2,1,0:T(8,128)(2,1)}, bf16[2,8,48,384]{3,2,1,0:T(8,128)(2,1)}, u32[]{:S(2)}, u32[]{:S(2)}) collective-permute-start(bf16[2,8,48,384]{3,2,1,0:T(8,128)(2,1)} %fusion.28), channel_id=1, source_target_pairs={{0,1},{1,0},{2,3},{3,2},{4,5},{5,4},{6,7},{7,6},{8,9},{9,8},{10,11... | collective-permute-start | bytes 1769480 | tf_op jit(solution)/shard_map/ppermute | solution.py:1004
  386.7 17.4 %copy-start.12 = (bf16[128,1536]{1,0:T(8,128)(2,1)S(1)}, bf16[128,1536]{1,0:T(8,128)(2,1)}, u32[]{:S(2)}) copy-start(bf16[128,1536]{1,0:T(8,128)(2,1)} %tok.1) | copy-start | bytes 1179652
  386.7 17.4 %copy-start.62 = (f32[128]{0:T(128)S(1)}, f32[128]{0:T(128)}, u32[]{:S(2)}) copy-start(f32[128]{0:T(128)} %get-tuple-element.122) | copy-start | bytes 1540
  386.7 17.9 %copy-start.26 = (bf16[128,1536]{1,0:T(8,128)(2,1)S(1)}, bf16[128,1536]{1,0:T(8,128)(2,1)}, u32[]{:S(2)}) copy-start(bf16[128,1536]{1,0:T(8,128)(2,1)} %cot.1) | copy-start | bytes 1179652
  386.7 17.9 %copy-start.55 = (f32[1536]{0:T(1024)S(1)}, f32[1536]{0:T(1024)}, u32[]{:S(2)}) copy-start(f32[1536]{0:T(1024)} %copy-done.53) | copy-start | bytes 18436
  386.7 17.9 %copy-start.61 = (f32[128]{0:T(128)S(1)}, f32[128]{0:T(128)}, u32[]{:S(2)}) copy-start(f32[128]{0:T(128)} %copy-done.59) | copy-start | bytes 1540
  386.7 17.9 %copy-start.64 = (f32[128]{0:T(128)S(1)}, f32[128]{0:T(128)}, u32[]{:S(2)}) copy-start(f32[128]{0:T(128)} %broadcast_multiply_fusion.1) | copy-start | bytes 1540
  409.2 44.2 %collective-permute-start.14 = (bf16[128,1536]{1,0:T(8,128)(2,1)S(1)}, bf16[128,1536]{1,0:T(8,128)(2,1)S(1)}, u32[]{:S(2)}, u32[]{:S(2)}) collective-permute-start(bf16[128,1536]{1,0:T(8,128)(2,1)S(1)} %fusion.33), channel_id=1, source_target_pairs={{0,16},{2,18},{4,20},{6,22},{8,24},{10,26},{12,28},{14,30},{16,0},... | collective-permute-start | bytes 1179656 | tf_op jit(solution)/shard_map/ppermute | solution.py:1008
  409.3 6.2 %copy-start.46 = (f32[2,8,2,48,384]{4,3,2,1,0:T(8,128)S(1)}, f32[2,8,2,48,384]{4,3,2,1,0:T(8,128)}, u32[]{:S(2)}) copy-start(f32[2,8,2,48,384]{4,3,2,1,0:T(8,128)} %copy-done.45) | copy-start | bytes 7077892
  412.5 4.3 copy-start.56
  412.5 64.3 %collective-permute-start.9 = (bf16[8,48,1024]{2,1,0:T(8,128)(2,1)S(1)}, bf16[8,48,1024]{2,1,0:T(8,128)(2,1)S(1)}, u32[]{:S(2)}, u32[]{:S(2)}) collective-permute-start(bf16[8,48,1024]{2,1,0:T(8,128)(2,1)S(1)} %fusion.23), channel_id=1, source_target_pairs={{0,16},{2,18},{4,20},{6,22},{8,24},{10,26},{12,28},{14,30},{16,0},... | collective-permute-start | bytes 2359304 | tf_op jit(solution)/shard_map/ppermute | solution.py:1008
  416.8 59.3 %collective-permute-start.11 = (bf16[8,48,384]{2,1,0:T(8,128)(2,1)S(1)}, bf16[8,48,384]{2,1,0:T(8,128)(2,1)S(1)}, u32[]{:S(2)}, u32[]{:S(2)}) collective-permute-start(bf16[8,48,384]{2,1,0:T(8,128)(2,1)S(1)} %fusion.35), channel_id=1, source_target_pairs={{0,16},{2,18},{4,20},{6,22},{8,24},{10,26},{12,28},{14,30},{16,0},... | collective-permute-start | bytes 884744 | tf_op jit(solution)/shard_map/ppermute | solution.py:1008
  453.4 23.4 %copy-start.43 = (bf16[128,1536]{1,0:T(8,128)(2,1)}, bf16[128,1536]{1,0:T(8,128)(2,1)S(1)}, u32[]{:S(2)}) copy-start(bf16[128,1536]{1,0:T(8,128)(2,1)S(1)} %collective-permute-done.14) | copy-start | bytes 1179652
  511.8 26.9 %copy-start.63 = (f32[2,48]{1,0:T(2,128)}, f32[2,48]{1,0:T(2,128)S(1)}, u32[]{:S(2)}) copy-start(f32[2,48]{1,0:T(2,128)S(1)} %slice_reduce_fusion) | copy-start | bytes 1156
  516.1 23.2 %copy-start.30 = (f32[48,1536]{1,0:T(8,128)}, f32[48,1536]{1,0:T(8,128)S(1)}, u32[]{:S(2)}) copy-start(f32[48,1536]{1,0:T(8,128)S(1)} %convert_reduce_fusion) | copy-start | bytes 884740
  538.7 6.3 %copy-start.16 = (f32[1,48,8192]{2,1,0:T(8,128)}, f32[1,48,8192]{2,1,0:T(8,128)S(1)}, u32[]{:S(2)}) copy-start(f32[1,48,8192]{2,1,0:T(8,128)S(1)} %reshape.896) | copy-start | bytes 4718596
  538.8 3.4 copy-start.32
  538.8 3.3 copy-start.33
  538.8 3.3 copy-start.50
  539.4 5.6 %copy-start.42 = (f32[1,48,8192]{2,1,0:T(8,128)S(1)}, f32[1,48,8192]{2,1,0:T(8,128)}, u32[]{:S(2)}) copy-start(f32[1,48,8192]{2,1,0:T(8,128)} %param.33) | copy-start | bytes 4718596
  545.0 3.3 copy-start.29
  545.0 3.3 copy-start.44
  545.0 3.3 copy-start.48
  545.0 3.3 copy-start.49
  (29 other events, 48.0 us)

commit v2 on v1

--- a/solution.py
+++ b/solution.py
@@ -1,3 +1,5 @@
+import functools
+
 import jax
 import jax.numpy as jnp
 from jax import lax
@@ -470,7 +472,8 @@
 SEQ = 16
 FLEET = 32
 ROWS = 128
-HALF_ROWS = 64
+TOP_ROWS = 64
+DOC_KINDS = 6
 KEYS = 1024
 BLOCK = 256
 CORE, NEAR_Y, NEAR_Z = 1, 2, 4
@@ -504,8 +507,8 @@
         rank = lax.rem(self.rank + step, FLEET)
         return rank, (lax.div(rank, 2), lax.rem(rank, 2))
 
-    def before(self, step):
-        return lax.rem(self.rank + FLEET - step, FLEET)
+    def twin(self):
+        return (self.seq, 1 - self.fsdp)
 
 
 def send(src, dst, sems, index, device):
@@ -533,12 +536,12 @@
 class SquareGather:
     COPIES = 10
 
-    def __init__(self, place, src, out, sems, local_sem):
-        p, h = place, HALF_ROWS
+    def __init__(self, place, src, out, sems, local_sem, top_rows):
+        p, h = place, top_rows
         own, ys, zs = p.slot(0), p.slot(NEAR_Y), p.slot(NEAR_Z)
         ds = p.slot(NEAR_Y | NEAR_Z)
         to_y, to_z, to_c = p.peer(NEAR_Y), p.peer(NEAR_Z), p.peer(CORE)
-        top, low = pl.ds(0, h), pl.ds(h, h)
+        top, low = pl.ds(0, h), pl.ds(h, ROWS - h)
         self.local = pltpu.make_async_copy(src, out.at[own], local_sem)
         self.y0 = send(src.at[top], out.at[own, top], sems, 0, to_y)
         self.y1 = send(src.at[low], out.at[own, low], sems, 1, to_y)
@@ -580,109 +583,30 @@
         self.local.wait()
 
 
-def first_kernel(tok, cot, gain, mix, inn, out, tok_o, cot_o, gain_o, mix_o, inn_o, out_o, *sems):
-    place = Place()
-    tok_s, cot_s, gain_s, mix_s, inn_s, out_s = (sems[2 * i : 2 * i + 2] for i in range(6))
-    local_sem = sems[12]
-    greet([place.after(step)[1] for step in range(1, FLEET)])
-    gather_tok = SquareGather(place, tok, tok_o, tok_s, local_sem.at[0])
-    gather_cot = SquareGather(place, cot, cot_o, cot_s, local_sem.at[1])
-    gather_tok.start()
-    copies = []
-    for step in range(1, FLEET):
-        rank, device = place.after(step)
-        column = lax.rem(device[0], SQUARE)
-        copies.append(send(gain, gain_o.at[place.rank], gain_s, step, device))
-        copies.append(send(mix.at[column], mix_o.at[place.rank], mix_s, step, device))
-    locals_ = [
-        pltpu.make_async_copy(gain, gain_o.at[place.rank], local_sem.at[2]),
-        pltpu.make_async_copy(mix.at[place.member], mix_o.at[place.rank], local_sem.at[3]),
-        pltpu.make_async_copy(inn.at[place.member], inn_o.at[place.member], local_sem.at[4]),
+def mix_spread(place, mix, mix_o, plane_s, cross_s, local_sem):
+    twin = (place.seq, 1 - place.fsdp)
+    first = [
+        send(
+            mix.at[lax.rem(flip(place.seq, bits), SQUARE)],
+            mix_o.at[place.rank],
+            plane_s,
+            bits,
+            (flip(place.seq, bits), place.fsdp),
+        )
+        for bits in range(1, SEQ)
     ]
-    for bits in range(1, SQUARE):
-        copies.append(
-            send(inn.at[place.slot(bits)], inn_o.at[place.member], inn_s, bits, place.peer(bits))
-        )
-    for copy in copies + locals_:
-        copy.start()
-    keeper = lax.div(place.seq, 2)
-    spot = lax.rem(place.seq, 2) * 2 + place.fsdp
-
-    def out_copy(number):
-        device = ((number // 2) * SQUARE + keeper, number % 2)
-        remote = pltpu.make_async_remote_copy(
-            src_ref=out,
-            dst_ref=out_o.at[spot],
-            send_sem=out_s[0].at[number],
-            recv_sem=out_s[1].at[spot],
-            device_id=device,
-            device_id_type=MESH,
-        )
-        local = pltpu.make_async_copy(out, out_o.at[spot], local_sem.at[5])
-        mine = (device[0] == place.seq) & (device[1] == place.fsdp)
-        return remote, local, mine
-
-    for number in range(4):
-        remote, local, mine = out_copy(number)
-        pl.when(mine)(local.start)
-        pl.when(jnp.logical_not(mine))(remote.start)
-    gather_tok.relay()
-    gather_tok.share()
-    gather_cot.start()
-    gather_cot.relay()
-    gather_cot.share()
-    gather_tok.finish()
-    gather_cot.finish()
-    for copy in copies + locals_:
-        copy.wait()
-    for number in range(4):
-        remote, local, mine = out_copy(number)
-        pl.when(mine)(local.wait)
-        pl.when(jnp.logical_not(mine))(remote.wait_send)
-    for number in range(4):
-        source_seq = place.member * 2 + number // 2
-        mine = (source_seq == place.seq) & (number % 2 == place.fsdp)
-        arrival = pltpu.make_async_remote_copy(
-            src_ref=out,
-            dst_ref=out_o.at[number],
-            send_sem=out_s[0].at[number],
-            recv_sem=out_s[1].at[number],
-            device_id=(source_seq, number % 2),
-            device_id_type=MESH,
-        )
-        pl.when(jnp.logical_not(mine))(arrival.wait_recv)
-
-
-def first_exchange(tok, cot, gain, mix, inn, out):
-    shape = jax.ShapeDtypeStruct
-    return pl.pallas_call(
-        first_kernel,
-        out_shape=(
-            shape((SQUARE,) + tok.shape, LOW),
-            shape((SQUARE,) + cot.shape, LOW),
-            shape((FLEET,) + gain.shape, gain.dtype),
-            shape((FLEET,) + mix.shape[1:], LOW),
-            shape(inn.shape, LOW),
-            shape((4,) + out.shape, LOW),
-        ),
-        in_specs=[ANY] * 6,
-        out_specs=(ANY,) * 6,
-        scratch_shapes=pair_sems(SquareGather.COPIES)
-        + pair_sems(SquareGather.COPIES)
-        + pair_sems(FLEET)
-        + pair_sems(FLEET)
-        + pair_sems(SQUARE)
-        + pair_sems(4)
-        + [pltpu.SemaphoreType.DMA((6,))],
-        compiler_params=pltpu.CompilerParams(collective_id=0, has_side_effects=True),
-        name="first_exchange",
-    )(tok, cot, gain, mix, inn, out)
+    second = []
+    for bits in range(SEQ):
+        spot = flip(place.seq, bits) * 2 + place.fsdp
+        second.append(send(mix_o.at[spot], mix_o.at[spot], cross_s, bits, twin))
+    local = pltpu.make_async_copy(mix.at[place.member], mix_o.at[place.rank], local_sem)
+    return first, second, local
 
 
 def gather_kernel(src, out, send_sems, recv_sems, local_sem):
     place = Place()
     greet([place.peer(bits) for bits in (CORE, NEAR_Y, NEAR_Z)])
-    gather = SquareGather(place, src, out, (send_sems, recv_sems), local_sem.at[0])
+    gather = SquareGather(place, src, out, (send_sems, recv_sems), local_sem.at[0], TOP_ROWS)
     gather.start()
     gather.relay()
     gather.share()
@@ -714,54 +638,83 @@
     lax.fori_loop(0, count // step, body, 0)
 
 
-def scatter_kernel(part, total, sib, away, passed, landed, send_sems, recv_sems):
+class SquareScatter:
+    def __init__(self, place, part, total, buffers, sems, top_rows):
+        sib, away, passed, landed = buffers
+        self.place, self.part, self.total = place, part, total
+        self.sib, self.away, self.passed, self.landed = sib, away, passed, landed
+        h = self.top_rows = top_rows
+        top, low = pl.ds(0, h), pl.ds(h, ROWS - h)
+        to_y, to_z, to_c = place.peer(NEAR_Y), place.peer(NEAR_Z), place.peer(CORE)
+        self.order = (NEAR_Y | NEAR_Z, NEAR_Y, NEAR_Z, 0)
+        self.cores = [
+            send(part.at[place.slot(bits | CORE)], sib.at[number], sems, number, to_c)
+            for number, bits in enumerate(self.order)
+        ]
+        self.d0 = send(away.at[0, top], passed.at[top], sems, 4, to_y)
+        self.d1 = send(away.at[0, low], passed.at[low], sems, 5, to_z)
+        self.y0 = send(away.at[1, top], landed.at[0, top], sems, 6, to_y)
+        self.y1 = send(away.at[1, low], landed.at[0, low], sems, 7, to_y)
+        self.z0 = send(away.at[2, top], landed.at[1, top], sems, 8, to_z)
+        self.z1 = send(away.at[2, low], landed.at[1, low], sems, 9, to_z)
+
+    @staticmethod
+    def buffers(width):
+        return [
+            pltpu.VMEM((4, ROWS, width), LOW),
+            pltpu.VMEM((3, ROWS, width), LOW),
+            pltpu.VMEM((ROWS, width), LOW),
+            pltpu.VMEM((2, ROWS, width), LOW),
+        ]
+
+    @staticmethod
+    def scratch(width):
+        return SquareScatter.buffers(width) + pair_sems(10)
+
+    def start(self):
+        for copy in self.cores:
+            copy.start()
+
+    def pair_up(self):
+        for number, bits in enumerate(self.order):
+            self.cores[number].wait_recv()
+            target = self.away.at[number] if number < 3 else self.total
+            add_rows(target, self.part.at[self.place.slot(bits)], self.sib.at[number], 0, ROWS)
+            for copy in ((self.d0, self.d1), (self.y0,), (self.z1,), ())[number]:
+                copy.start()
+
+    def relay(self):
+        h, rest = self.top_rows, ROWS - self.top_rows
+        self.d0.wait_recv()
+        add_rows(self.away.at[2], self.away.at[2], self.passed, 0, h)
+        self.z0.start()
+        self.d1.wait_recv()
+        add_rows(self.away.at[1], self.away.at[1], self.passed, h, rest)
+        self.y1.start()
+
+    def finish(self):
+        h, rest = self.top_rows, ROWS - self.top_rows
+        total, landed = self.total, self.landed
+        self.y0.wait_recv()
+        add_rows(total, total, landed.at[0], 0, h)
+        self.z1.wait_recv()
+        add_rows(total, total, landed.at[1], h, rest)
+        self.z0.wait_recv()
+        add_rows(total, total, landed.at[1], 0, h)
+        self.y1.wait_recv()
+        add_rows(total, total, landed.at[0], h, rest)
+        for copy in self.cores + [self.d0, self.d1, self.y0, self.y1, self.z0, self.z1]:
+            copy.wait_send()
+
+
+def scatter_kernel(part, total, *scratch):
     place = Place()
-    sems = (send_sems, recv_sems)
     greet([place.peer(bits) for bits in (CORE, NEAR_Y, NEAR_Z)])
-    h = HALF_ROWS
-    top, low = pl.ds(0, h), pl.ds(h, h)
-    far = NEAR_Y | NEAR_Z
-    to_y, to_z, to_c = place.peer(NEAR_Y), place.peer(NEAR_Z), place.peer(CORE)
-    cores = [
-        send(part.at[place.slot(bits | CORE)], sib.at[number], sems, number, to_c)
-        for number, bits in enumerate((far, NEAR_Y, NEAR_Z, 0))
-    ]
-    for copy in cores:
-        copy.start()
-    d0 = send(away.at[0, top], passed.at[top], sems, 4, to_y)
-    d1 = send(away.at[0, low], passed.at[low], sems, 5, to_z)
-    y0 = send(away.at[1, top], landed.at[0, top], sems, 6, to_y)
-    y1 = send(away.at[1, low], landed.at[0, low], sems, 7, to_y)
-    z0 = send(away.at[2, top], landed.at[1, top], sems, 8, to_z)
-    z1 = send(away.at[2, low], landed.at[1, low], sems, 9, to_z)
-    cores[0].wait_recv()
-    add_rows(away.at[0], part.at[place.slot(far)], sib.at[0], 0, ROWS)
-    d0.start()
-    d1.start()
-    cores[1].wait_recv()
-    add_rows(away.at[1], part.at[place.slot(NEAR_Y)], sib.at[1], 0, ROWS)
-    y0.start()
-    cores[2].wait_recv()
-    add_rows(away.at[2], part.at[place.slot(NEAR_Z)], sib.at[2], 0, ROWS)
-    z1.start()
-    cores[3].wait_recv()
-    add_rows(total, part.at[place.slot(0)], sib.at[3], 0, ROWS)
-    d0.wait_recv()
-    add_rows(away.at[2], away.at[2], passed, 0, h)
-    z0.start()
-    d1.wait_recv()
-    add_rows(away.at[1], away.at[1], passed, h, h)
-    y1.start()
-    y0.wait_recv()
-    z1.wait_recv()
-    add_rows(total, total, landed.at[0], 0, h)
-    add_rows(total, total, landed.at[1], h, h)
-    z0.wait_recv()
-    add_rows(total, total, landed.at[1], 0, h)
-    y1.wait_recv()
-    add_rows(total, total, landed.at[0], h, h)
-    for copy in cores + [d0, d1, y0, y1, z0, z1]:
-        copy.wait_send()
+    scatter = SquareScatter(place, part, total, scratch[:4], scratch[4:], TOP_ROWS)
+    scatter.start()
+    scatter.pair_up()
+    scatter.relay()
+    scatter.finish()
 
 
 def square_scatter(part):
@@ -771,13 +724,7 @@
         out_shape=jax.ShapeDtypeStruct((ROWS, width), jnp.float32),
         in_specs=[VMEM],
         out_specs=VMEM,
-        scratch_shapes=[
-            pltpu.VMEM((4, ROWS, width), LOW),
-            pltpu.VMEM((3, ROWS, width), LOW),
-            pltpu.VMEM((ROWS, width), LOW),
-            pltpu.VMEM((2, ROWS, width), LOW),
-        ]
-        + pair_sems(10),
+        scratch_shapes=SquareScatter.scratch(width),
         compiler_params=pltpu.CompilerParams(
             collective_id=2, has_side_effects=True, vmem_limit_bytes=32 << 20
         ),
@@ -785,26 +732,59 @@
     )(part.reshape(SQUARE, ROWS, width))
 
 
-def last_kernel(inn, mix, out, gain, inn_o, mix_o, out_o, gain_o, *sems):
+def return_kernel(pair, part, pair_o, total, *scratch):
     place = Place()
-    inn_s, mix_s, out_s, gain_s = (sems[2 * i : 2 * i + 2] for i in range(4))
-    local_sem = sems[8]
-    greet([place.after(step)[1] for step in range(1, FLEET)])
-    copies = []
-    for bits in range(1, SQUARE):
-        peer, slot = place.peer(bits), place.slot(bits)
-        copies.append(send(mix.at[slot], mix_o.at[place.member], mix_s, bits, peer))
-        copies.append(send(inn.at[slot], inn_o.at[place.member], inn_s, bits, peer))
-    for step in range(1, FLEET):
-        rank, device = place.after(step)
-        copies.append(send(gain.at[rank], gain_o.at[place.rank], gain_s, step, device))
-    copies += [
-        pltpu.make_async_copy(inn.at[place.member], inn_o.at[place.member], local_sem.at[0]),
-        pltpu.make_async_copy(mix.at[place.member], mix_o.at[place.member], local_sem.at[1]),
-        pltpu.make_async_copy(gain.at[place.rank], gain_o.at[place.rank], local_sem.at[2]),
+    greet([place.peer(bits) for bits in (CORE, NEAR_Y, NEAR_Z, SQUARE)])
+    down = send(pair, pair_o, scratch[:2], 0, place.peer(SQUARE))
+    pl.when(place.half == 1)(down.start)
+    scatter = SquareScatter(place, part, total, scratch[2:6], scratch[6:], TOP_ROWS)
+    scatter.start()
+    scatter.pair_up()
+    scatter.relay()
+    scatter.finish()
+    pl.when(place.half == 1)(down.wait_send)
+    pl.when(place.half == 0)(down.wait_recv)
+
+
+def return_exchange(pair, part):
+    width = part.shape[-1]
+    shape = jax.ShapeDtypeStruct
+    return pl.pallas_call(
+        return_kernel,
+        out_shape=(shape(pair.shape, LOW), shape((ROWS, width), jnp.float32)),
+        in_specs=[ANY, VMEM],
+        out_specs=(ANY, VMEM),
+        scratch_shapes=pair_sems(1) + SquareScatter.scratch(width),
+        compiler_params=pltpu.CompilerParams(
+            collective_id=6, has_side_effects=True, vmem_limit_bytes=32 << 20
+        ),
+        name="return_exchange",
+    )(pair, part.reshape(SQUARE, ROWS, width))
+
+
+def last_kernel(
+    part, mix, inn, out, total, mix_o, inn_o, out_o, crossed, staged, landed, *scratch
+):
+    place = Place()
+    cross_s, plane_s, inn_s, out_s = (scratch[2 * i : 2 * i + 2] for i in range(4))
+    local_sem = scratch[8]
+    greet([(flip(place.seq, bits), place.fsdp) for bits in range(1, SEQ)] + [place.twin()])
+    twin = place.twin()
+    order = list(range(SEQ - 1, -1, -1))
+    cross = {}
+    for bits in order:
+        target = flip(place.seq, bits)
+        cross[bits] = send(mix.at[target, 1 - place.fsdp], crossed.at[target], cross_s, bits, twin)
+        cross[bits].start()
+    scatter = SquareScatter(place, part, total, scratch[9:13], scratch[13:], TOP_ROWS)
+    scatter.start()
+    copies = [
+        send(inn.at[place.slot(bits)], inn_o.at[place.member], inn_s, bits, place.peer(bits))
+        for bits in range(1, SQUARE)
     ]
-    for copy in copies:
-        copy.start()
+    copies.append(
+        pltpu.make_async_copy(inn.at[place.member], inn_o.at[place.member], local_sem.at[0])
+    )
 
     def out_copy(number):
         owner = place.member * 2 + number
@@ -816,13 +796,42 @@
             device_id=(owner, place.fsdp),
             device_id_type=MESH,
         )
-        local = pltpu.make_async_copy(out.at[number], out_o.at[place.half], local_sem.at[3])
+        local = pltpu.make_async_copy(out.at[number], out_o.at[place.half], local_sem.at[1])
         return remote, local, owner == place.seq
 
+    scatter.pair_up()
     for number in range(2):
         remote, local, mine = out_copy(number)
         pl.when(mine)(local.start)
         pl.when(jnp.logical_not(mine))(remote.start)
+    plane = {}
+    for bits in order:
+        target = flip(place.seq, bits)
+        cross[bits].wait_recv()
+        goal = staged.at[target] if bits else landed.at[place.seq]
+        add_rows(goal, mix.at[target, place.fsdp], crossed.at[target], 0, mix.shape[2])
+        if bits:
+            plane[bits] = send(
+                staged.at[target], landed.at[place.seq], plane_s, bits, (target, place.fsdp)
+            )
+            plane[bits].start()
+        if bits == SQUARE:
+            scatter.relay()
+            for copy in copies:
+                copy.start()
+    scatter.finish()
+    for bits in range(1, SEQ):
+        plane[bits].wait_recv()
+
+    def body(member, _):
+        add_rows(mix_o.at[member], landed.at[member], landed.at[member + SQUARE], 0, mix.shape[2])
+        return 0
+
+    lax.fori_loop(0, SQUARE, body, 0)
+    for bits in order:
+        cross[bits].wait_send()
+        if bits:
+            plane[bits].wait_send()
     for copy in copies:
         copy.wait()
     for number in range(2):
@@ -842,47 +851,74 @@
         pl.when(source_seq != place.seq)(arrival.wait_recv)
 
 
-def last_exchange(inn, mix, out, gain):
+def last_exchange(part, mix, inn, out):
     shape = jax.ShapeDtypeStruct
+    width = part.shape[-1]
+    share, columns = mix.shape[2:]
     return pl.pallas_call(
         last_kernel,
-        out_shape=tuple(shape(v.shape, v.dtype) for v in (inn, mix, out, gain)),
-        in_specs=[ANY] * 4,
-        out_specs=(ANY,) * 4,
-        scratch_shapes=pair_sems(SQUARE)
+        out_shape=(
+            shape((ROWS, width), jnp.float32),
+            shape((SQUARE, share, columns), jnp.float32),
+            shape(inn.shape, LOW),
+            shape(out.shape, LOW),
+        ),
+        in_specs=[VMEM, VMEM, ANY, ANY],
+        out_specs=(VMEM, VMEM, ANY, ANY),
+        scratch_shapes=[pltpu.VMEM((SEQ, share, columns), LOW)] * 3
+        + pair_sems(SEQ)
+        + pair_sems(SEQ)
         + pair_sems(SQUARE)
         + pair_sems(2)
-        + pair_sems(FLEET)
-        + [pltpu.SemaphoreType.DMA((4,))],
-        compiler_params=pltpu.CompilerParams(collective_id=3, has_side_effects=True),
+        + [pltpu.SemaphoreType.DMA((2,))]
+        + SquareScatter.scratch(width),
+        compiler_params=pltpu.CompilerParams(
+            collective_id=3, has_side_effects=True, vmem_limit_bytes=40 << 20
+        ),
         name="last_exchange",
-    )(inn, mix, out, gain)
-
-
-def share_kernel(value, out, send_sems, recv_sems):
+    )(part.reshape(SQUARE, ROWS, width), mix, inn, out)
+
+
+def norm_kernel(gain, squares, gain_o, total_o, gains, sums, mine, *sems):
     place = Place()
+    gain_s, sum_s = sems[0:2], sems[2:4]
     greet([place.after(step)[1] for step in range(1, FLEET)])
-    out[place.rank] = value[...]
     copies = []
     for step in range(1, FLEET):
         rank, device = place.after(step)
-        copies.append(send(value, out.at[place.rank], (send_sems, recv_sems), step, device))
-    for copy in copies:
-        copy.start()
+        copies.append(send(gain.at[rank], gains.at[place.rank], gain_s, step, device))
+        copies[-1].start()
+    gains[place.rank] = gain[place.rank]
     for copy in copies:
         copy.wait()
-
-
-def share_all(value):
+    total = jnp.sum(gains[...], axis=0)
+    gain_o[...] = total
+    mine[...] = squares[...] + total * total
+    copies = []
+    for step in range(1, FLEET):
+        rank, device = place.after(step)
+        copies.append(send(mine, sums.at[place.rank], sum_s, step, device))
+        copies[-1].start()
+    sums[place.rank] = mine[...]
+    for copy in copies:
+        copy.wait()
+    total_o[...] = jnp.sum(sums[...], axis=0)
+
+
+def norm_exchange(gain, squares):
+    shape = jax.ShapeDtypeStruct
     return pl.pallas_call(
-        share_kernel,
-        out_shape=jax.ShapeDtypeStruct((FLEET,) + value.shape, value.dtype),
-        in_specs=[VMEM],
-        out_specs=VMEM,
-        scratch_shapes=pair_sems(FLEET),
+        norm_kernel,
+        out_shape=(shape(gain.shape[1:], jnp.float32), shape(squares.shape, jnp.float32)),
+        in_specs=[VMEM] * 2,
+        out_specs=(VMEM,) * 2,
+        scratch_shapes=[pltpu.VMEM(gain.shape, jnp.float32)] * 2
+        + [pltpu.VMEM(squares.shape, jnp.float32)]
+        + pair_sems(FLEET)
+        + pair_sems(FLEET),
         compiler_params=pltpu.CompilerParams(collective_id=4, has_side_effects=True),
-        name="share_all",
-    )(value)
+        name="norm_exchange",
+    )(gain, squares)
 
 
 def dot32(left, right, dims=((1,), (0,))):
@@ -899,51 +935,448 @@
     return key_at > query_at
 
 
-def attend_kernel(half, query_t, keys, values_t, out_t, log_sum):
-    first = jnp.where(half[0] == 1, 0, KEYS // BLOCK)
-    for number in range(KEYS // BLOCK):
+class Mailbox:
+    def __init__(self, sends, receives, locals_):
+        self.sends, self.receives, self.locals_ = sends, receives, locals_
+        self.taken, self.local_taken = 0, 0
+
+    def take(self, count):
+        start = self.taken
+        self.taken += count
+        spot = pl.ds(start, count)
+        return (self.sends.at[spot], self.receives.at[spot])
+
+    def local(self):
+        self.local_taken += 1
+        return self.locals_.at[self.local_taken - 1]
+
+
+def token_layout(lengths, group, start, count):
+    at = start + lax.broadcasted_iota(jnp.int32, (1, count), 1)
+    segment = jnp.zeros((1, count), jnp.int32)
+    offset = jnp.zeros((1, count), jnp.int32)
+    end = jnp.int32(0)
+    for number in range(lengths.shape[1]):
+        length = lengths[group, number]
+        end = end + length
+        passed = (at >= end).astype(jnp.int32)
+        segment = segment + passed
+        offset = offset + passed * length
+    return segment, at - offset
+
+
+def wall_rows(segment):
+    kind = lax.broadcasted_iota(jnp.int32, (32, segment.shape[1]), 0)
+    return jnp.where((kind != segment) & (kind < DOC_KINDS), -WALL, 0.0)
+
+
+def mark_rows(segment):
+    kind = lax.broadcasted_iota(jnp.int32, (32, segment.shape[1]), 0)
+    return jnp.where(kind == segment, 1.0, 0.0)
+
+
+def turn_head(head, cosine, sine):
+    former, latter = head[: HEAD_DIM // 2], head[HEAD_DIM // 2 :]
+    return jnp.concatenate(
+        [former * cosine - latter * sine, latter * cosine + former * sine], axis=0
+    )
+
+
+class WeightSpread:
+    CHUNKS = 4
+
+    def __init__(self, place, inn, down, in_o, down_o, mail):
+        p = place
+        twin, across = p.twin(), p.peer(SQUARE)
+        self.square = [
+            send(inn.at[p.slot(bits)], in_o.at[p.half, p.member, p.fsdp], box, 0, p.peer(bits))
+            for bits in range(1, SQUARE)
+            for box in (mail.take(1),)
+        ]
+        self.local = pltpu.make_async_copy(
+            inn.at[p.member], in_o.at[p.half, p.member, p.fsdp], mail.local()
+        )
+        self.down_local = pltpu.make_async_copy(down, down_o.at[p.half, p.fsdp], mail.local())
+        near = in_o.at[p.half, pl.ds(0, SQUARE), p.fsdp]
+        self.near = send(near, near, mail.take(1), 0, twin)
+        width = SQUARE // self.CHUNKS
+        self.far, self.passed = [], []
+        boxes, passed_boxes = mail.take(self.CHUNKS), mail.take(self.CHUNKS)
+        for number in range(self.CHUNKS):
+            rows = pl.ds(number * width, width)
+            mine = in_o.at[p.half, rows, p.fsdp]
+            other = in_o.at[1 - p.half, rows, p.fsdp]
+            self.far.append(send(mine, mine, boxes, number, across))
+            self.passed.append(send(other, other, passed_boxes, number, twin))
+        boxes = mail.take(3)
+        self.down_near = send(down, down_o.at[p.half, p.fsdp], boxes, 0, twin)
+        self.down_far = send(down, down_o.at[p.half, p.fsdp], boxes, 1, across)
+        other = down_o.at[1 - p.half, p.fsdp]
+        self.down_passed = send(other, other, boxes, 2, twin)
+
+    def start_square(self):
+        for copy in self.square:
+            copy.start()
+        self.local.start()
+
+    def square_done(self):
+        for copy in self.square:
+            copy.wait_recv()
+        self.local.wait()
+
+    def pass_on(self, number):
+        self.far[number].wait_recv()
+        self.passed[number].start()
+
+    def finish(self):
+        for copy in self.square + self.far:
+            copy.wait_send()
+        for copy in self.passed + [self.near]:
+            copy.wait()
+        self.down_far.wait_send()
+        self.down_near.wait()
+        self.down_passed.wait()
+        self.down_local.wait()
+
+
+def forward_kernel(
+    lengths,
+    frequency,
+    tok,
+    gain,
+    mix,
+    out,
+    inn,
+    down,
+    mix_o,
+    out_o,
+    in_o,
+    down_o,
+    gain_o,
+    normed_o,
+    query_o,
+    keys_o,
+    values_o,
+    pair_o,
+    att_o,
+    log_o,
+    cos_o,
+    sin_o,
+    middle_o,
+    two_o,
+    tok_all,
+    gains,
+    top_s,
+    sum_s,
+    mixed_s,
+    att_low,
+    part,
+    two,
+    sib,
+    away,
+    passed,
+    landed,
+    sends,
+    receives,
+    locals_,
+):
+    f32 = jnp.float32
+    place = Place()
+    mail = Mailbox(sends, receives, locals_)
+    twin = place.twin()
+    blocks = KEYS // BLOCK
+    greet([place.after(step)[1] for step in range(1, FLEET)])
+    gather_tok = SquareGather(place, tok, tok_all, mail.take(10), mail.local(), TOP_ROWS)
+    first, second, mix_local = mix_spread(
+        place, mix, mix_o, mail.take(SEQ), mail.take(SEQ), mail.local()
+    )
+    mix_local.start()
+    for bits in range(SEQ - 1, SQUARE - 1, -1):
+        first[bits - 1].start()
+    gather_tok.start()
+    for bits in range(SQUARE - 1, 0, -1):
+        first[bits - 1].start()
+    gain_local = pltpu.make_async_copy(gain, gains.at[place.rank], mail.local())
+    gain_local.start()
+    gain_copies = []
+    boxes = mail.take(FLEET)
+    for step in range(1, FLEET):
+        rank, device = place.after(step)
+        gain_copies.append(send(gain, gains.at[place.rank], boxes, step, device))
+        gain_copies[-1].start()
+
+    keeper = lax.div(place.seq, 2)
+    spot = lax.rem(place.seq, 2)
+    out_boxes, out_local, twin_boxes = mail.take(2), mail.local(), mail.take(2)
+
+    def out_copy(number):
+        remote = pltpu.make_async_remote_copy(
+            src_ref=out,
+            dst_ref=out_o.at[spot, place.fsdp],
+            send_sem=out_boxes[0].at[number],
+            recv_sem=out_boxes[1].at[spot],
+            device_id=(number * SQUARE + keeper, place.fsdp),
+            device_id_type=MESH,
+        )
+        local = pltpu.make_async_copy(out, out_o.at[spot, place.fsdp], out_local)
+        return remote, local, number * SQUARE + keeper == place.seq
+
+    def out_arrival(number):
+        source = place.member * 2 + number
+        arrival = pltpu.make_async_remote_copy(
+            src_ref=out,
+            dst_ref=out_o.at[number, place.fsdp],
+            send_sem=out_boxes[0].at[number],
+            recv_sem=out_boxes[1].at[number],
+            device_id=(source, place.fsdp),
+            device_id_type=MESH,
+        )
+        return arrival, source == place.seq
+
+    for number in range(2):
+        remote, local, mine = out_copy(number)
+        pl.when(mine)(local.start)
+        pl.when(jnp.logical_not(mine))(remote.start)
+
+    segment, position = token_layout(lengths, place.fsdp, place.half * KEYS, KEYS)
+    angle = frequency[...] * position.astype(f32)
+    cos_o[...] = jnp.cos(angle)
+    sin_o[...] = jnp.sin(angle)
+    keep = (segment < lengths.shape[1]).astype(f32)
+    marks = mark_rows(segment).astype(LOW)
+    for head in range(2):
+        query_o[head, HEAD_DIM:, :] = marks
+    walls = wall_rows(segment)
+
+    gather_tok.relay()
+    mix_local.wait()
+    second[0].start()
+    for bits in range(SQUARE - 1, 0, -1):
+        first[bits - 1].wait_recv()
+        second[bits].start()
+    gather_tok.share()
+    for bits in range(SEQ - 1, SQUARE - 1, -1):
+        first[bits - 1].wait_recv()
+        second[bits].start()
+    spread = WeightSpread(place, inn, down, in_o, down_o, mail)
+    spread.down_local.start()
+    spread.down_near.start()
+    spread.down_far.start()
+    spread.start_square()
+    gain_local.wait()
+    for copy in gain_copies:
+        copy.wait()
+    gain_o[...] = jnp.zeros_like(gain_o)
+    for rank in range(FLEET):
+        lane = rank * (D // FLEET) // 128 * 128
+        gain_o[:, lane : lane + 256] += gains[rank].astype(f32)
+    gather_tok.finish()
+    for copy in second:
+        copy.wait_recv()
+
+    up_boxes = mail.take(blocks)
+    up = [
+        send(pair_o.at[blocks + number], pair_o.at[number], up_boxes, number, place.peer(SQUARE))
+        for number in range(blocks)
+    ]
+    for number in range(blocks):
         columns = pl.ds(number * BLOCK, BLOCK)
-        queries = jnp.concatenate([query_t[0, :, columns], query_t[1, :, columns]], axis=1)
-
-        def fold(place, carry, diagonal=False):
-            score = dot32(keys[block_of(place), :], queries)
-            if diagonal:
-                score = jnp.where(later(2 * BLOCK), -WALL, score)
-            top = jnp.max(score, axis=0, keepdims=True)
-            if carry is not None:
-                top = jnp.maximum(carry[0], top)
-            weight = jnp.exp2((score - top) * SCALE2)
-            total = jnp.sum(weight, axis=0, keepdims=True)
-            mixed = dot32(values_t[:, block_of(place)], weight.astype(LOW))
-            if carry is not None:
-                fade = jnp.exp2((carry[0] - top) * SCALE2)
-                total = total + carry[1] * fade
-                mixed = mixed + carry[2] * fade
-            return (top, total, mixed)
-
-        last = KEYS // BLOCK + number
-        carry = fold(last, None, diagonal=True)
-        top, total, mixed = lax.fori_loop(first, last, fold, carry)
+        halves = []
+        for block in (2 * number, 2 * number + 1):
+            x = tok_all[block].astype(f32)
+            scale = lax.rsqrt(jnp.mean(x * x, axis=-1, keepdims=True) + EPS_NORM)
+            low = (x * scale * gain_o[0:1, :D]).astype(LOW)
+            normed_o[block] = low
+            halves.append(dot32(low, mix_o[...].reshape(D, 4 * HEAD_DIM)).T)
+        projected = jnp.concatenate(halves, axis=1)
+        cosine, sine = cos_o[:, columns], sin_o[:, columns]
+        for head in range(2):
+            turned = turn_head(projected[head * HEAD_DIM : (head + 1) * HEAD_DIM], cosine, sine)
+            query_o[head, :HEAD_DIM, columns] = turned.astype(LOW)
+        key = turn_head(projected[2 * HEAD_DIM : 3 * HEAD_DIM], cosine, sine).astype(LOW)
+        value = projected[3 * HEAD_DIM :].astype(LOW)
+        pair_o[blocks + number, :HEAD_DIM] = key
+        pair_o[blocks + number, HEAD_DIM:] = value
+        pl.when(place.half == 0)(up[number].start)
+        rows = pl.ds(KEYS + number * BLOCK, BLOCK)
+        wall = walls[:, number * BLOCK : (number + 1) * BLOCK]
+        keys_o[rows, :] = jnp.concatenate([key.astype(f32), wall], axis=0).T.astype(LOW)
+        values_o[rows, :] = value.astype(f32).T.astype(LOW)
+
+    def queries_of(number):
+        columns = pl.ds(number * BLOCK, BLOCK)
+        return jnp.concatenate([query_o[0, :, columns], query_o[1, :, columns]], axis=1)
+
+    def fold(queries, spot, carry, diagonal=False):
+        score = dot32(keys_o[block_of(spot), :], queries)
+        if diagonal:
+            score = jnp.where(later(2 * BLOCK), -WALL, score)
+        top = jnp.max(score, axis=0, keepdims=True)
+        if carry is not None:
+            top = jnp.maximum(carry[0], top)
+        weight = jnp.exp2((score - top) * SCALE2)
+        total = jnp.sum(weight, axis=0, keepdims=True)
+        mixed = dot32(pair_o[spot, HEAD_DIM:], weight.astype(LOW))
+        if carry is not None:
+            fade = jnp.exp2((carry[0] - top) * SCALE2)
+            total = total + carry[1] * fade
+            mixed = mixed + carry[2] * fade
+        return (top, total, mixed)
+
+    for number in range(blocks):
+        queries = queries_of(number)
+        carry = fold(queries, blocks + number, None, diagonal=True)
+        carry = lax.fori_loop(
+            blocks, blocks + number, functools.partial(fold, queries), carry
+        )
+        top_s[number : number + 1, :], sum_s[number : number + 1, :] = carry[:2]
+        mixed_s[number] = carry[2]
+
+    spread.square_done()
+    spread.near.start()
+    for number in range(2):
+        remote, local, mine = out_copy(number)
+        pl.when(mine)(local.wait)
+        pl.when(jnp.logical_not(mine))(remote.wait_send)
+    passing = []
+    for number in range(2):
+        arrival, mine = out_arrival(number)
+        pl.when(jnp.logical_not(mine))(arrival.wait_recv)
+        block = out_o.at[number, place.fsdp]
+        passing.append(send(block, block, twin_boxes, number, twin))
+        passing[-1].start()
+    spread.down_far.wait_recv()
+    spread.down_passed.start()
+
+    @pl.when(place.half == 1)
+    def _():
+        other_segment, _ = token_layout(lengths, place.fsdp, 0, KEYS)
+        other_walls = wall_rows(other_segment)
+        for number in range(blocks):
+            up[number].wait_recv()
+            rows = pl.ds(number * BLOCK, BLOCK)
+            wall = other_walls[:, number * BLOCK : (number + 1) * BLOCK]
+            keys_o[rows, :] = (
+                jnp.concatenate([pair_o[number, :HEAD_DIM].astype(f32), wall], axis=0)
+                .T.astype(LOW)
+            )
+            values_o[rows, :] = pair_o[number, HEAD_DIM:].astype(f32).T.astype(LOW)
+
+    @pl.when(place.half == 0)
+    def _():
+        for number in range(blocks):
+            up[number].wait_send()
+            pair_o[number] = jnp.zeros_like(pair_o[number])
+        keys_o[pl.ds(0, KEYS), :] = jnp.zeros((KEYS, 128), LOW)
+        values_o[pl.ds(0, KEYS), :] = jnp.zeros((KEYS, HEAD_DIM), LOW)
+
+    for copy in spread.far:
+        copy.start()
+    for number in range(blocks):
+        columns = pl.ds(number * BLOCK, BLOCK)
+        carry = (top_s[number : number + 1, :], sum_s[number : number + 1, :], mixed_s[number])
+        carry = lax.fori_loop(
+            0,
+            jnp.where(place.half == 1, blocks, 0),
+            functools.partial(fold, queries_of(number)),
+            carry,
+        )
+        top, total, mixed = carry
         mixed = mixed * (1.0 / total)
         level = top * SCALE2 + jnp.log2(total)
         for head in range(2):
             side = slice(head * BLOCK, (head + 1) * BLOCK)
-            out_t[head, :, columns] = mixed[:, side]
-            log_sum[pl.ds(head, 1), columns] = level[:, side]
-
-
-def attend(half, query_t, keys, values_t):
+            rows = pl.ds(head * HEAD_DIM, HEAD_DIM)
+            kept = mixed[:, side] * keep[:, number * BLOCK : (number + 1) * BLOCK]
+            att_o[rows, columns] = kept
+            att_low[rows, columns] = kept.astype(LOW)
+            log_o[pl.ds(head, 1), columns] = level[:, side]
+
+    for copy in passing:
+        copy.wait_recv()
+    scatter = SquareScatter(
+        place, part, middle_o, (sib, away, passed, landed), mail.take(10), TOP_ROWS
+    )
+
+    def out_block(slot):
+        columns = pl.ds(pl.multiple_of(slot * ROWS, ROWS), ROWS)
+        rows = att_low[:, columns].astype(f32).T.astype(LOW)
+        part[slot] = dot32(rows, out_o[...].reshape(2 * HEAD_DIM, D)).astype(LOW)
+
+    for number, bits in enumerate(scatter.order):
+        out_block(place.slot(bits | CORE))
+        scatter.cores[number].start()
+    for bits in scatter.order:
+        out_block(place.slot(bits))
+    scatter.pair_up()
+    spread.pass_on(0)
+    scatter.relay()
+    scatter.finish()
+    middle = middle_o[...] + tok[...].astype(f32)
+    middle_o[...] = middle
+    scale = lax.rsqrt(jnp.mean(middle * middle, axis=-1, keepdims=True) + EPS_NORM)
+    two[...] = (middle * scale * gain_o[1:2, :D]).astype(LOW)
+    gather_two = SquareGather(place, two, two_o, mail.take(10), mail.local(), TOP_ROWS)
+    gather_two.start()
+    spread.pass_on(1)
+    gather_two.relay()
+    gather_two.share()
+    spread.pass_on(2)
+    gather_two.finish()
+    spread.pass_on(3)
+    spread.finish()
+    for copy in first + second + passing:
+        copy.wait_send()
+
+
+def forward(lengths, frequency, tok, gain, mix, out, inn, down):
+    shape = jax.ShapeDtypeStruct
+    f32 = jnp.float32
+    share, unit = out.shape[0], down.shape[0]
+    blocks = KEYS // BLOCK
     return pl.pallas_call(
-        attend_kernel,
+        forward_kernel,
         out_shape=(
-            jax.ShapeDtypeStruct((2, HEAD_DIM, KEYS), jnp.float32),
-            jax.ShapeDtypeStruct((2, KEYS), jnp.float32),
+            shape((FLEET,) + mix.shape[1:], LOW),
+            shape((2, 2) + out.shape, LOW),
+            shape((2, SQUARE, 2) + inn.shape[1:], LOW),
+            shape((2, 2) + down.shape, LOW),
+            shape((16, D + 128), f32),
+            shape((SQUARE, ROWS, D), LOW),
+            shape((2, 128, KEYS), LOW),
+            shape((2 * KEYS, 128), LOW),
+            shape((2 * KEYS, HEAD_DIM), LOW),
+            shape((2 * blocks, 2 * HEAD_DIM, BLOCK), LOW),
+            shape((2 * HEAD_DIM, KEYS), f32),
+            shape((2, KEYS), f32),
+            shape((HEAD_DIM // 2, KEYS), f32),
+            shape((HEAD_DIM // 2, KEYS), f32),
+            shape((ROWS, D), f32),
+            shape((SQUARE, ROWS, D), LOW),
         ),
-        in_specs=[pl.BlockSpec(memory_space=pltpu.SMEM)] + [VMEM] * 3,
-        out_specs=(VMEM, VMEM),
-        compiler_params=pltpu.CompilerParams(vmem_limit_bytes=40 << 20),
-        name="attend",
-    )(half, query_t, keys, values_t)
+        in_specs=[pl.BlockSpec(memory_space=pltpu.SMEM), VMEM, VMEM, VMEM] + [ANY] * 4,
+        out_specs=(VMEM, VMEM, ANY, ANY) + (VMEM,) * 12,
+        scratch_shapes=[
+            pltpu.VMEM((SQUARE, ROWS, D), LOW),
+            pltpu.VMEM((FLEET,) + gain.shape, LOW),
+            pltpu.VMEM((8, 2 * BLOCK), f32),
+            pltpu.VMEM((8, 2 * BLOCK), f32),
+            pltpu.VMEM((blocks, HEAD_DIM, 2 * BLOCK), f32),
+            pltpu.VMEM((2 * HEAD_DIM, KEYS), LOW),
+            pltpu.VMEM((SQUARE, ROWS, D), LOW),
+            pltpu.VMEM((ROWS, D), LOW),
+        ]
+        + SquareScatter.buffers(D)
+        + [
+            pltpu.SemaphoreType.DMA((160,)),
+            pltpu.SemaphoreType.DMA((160,)),
+            pltpu.SemaphoreType.DMA((16,)),
+        ],
+        compiler_params=pltpu.CompilerParams(
+            collective_id=0, has_side_effects=True, vmem_limit_bytes=56 << 20
+        ),
+        name="forward",
+    )(lengths, frequency, tok, gain, mix, out, inn, down)
 
 
 def attend_back_kernel(
@@ -1068,14 +1501,7 @@
     fsdp = lax.axis_index("fsdp")
     seq = lax.axis_index("seq")
     half, member = seq // SQUARE, seq % SQUARE
-    doc_lens = lax.dynamic_index_in_dim(lengths, fsdp, 0, keepdims=False)
-    places = half * KEYS + jnp.arange(KEYS, dtype=jnp.int32)
-    segment, positions = doc_layout(places, doc_lens)
-    other_segment, _ = doc_layout(jnp.arange(KEYS, dtype=jnp.int32), doc_lens)
-    keep_t = (segment < doc_lens.shape[0]).astype(f32)[None, :]
-    inverse = ROPE_BASE ** (-jnp.arange(HEAD_DIM // 2, dtype=f32) * 2.0 / HEAD_DIM)
-    angles = inverse[:, None] * positions.astype(f32)[None, :]
-    cosine, sine = jnp.cos(angles), jnp.sin(angles)
+    frequency = ROPE_BASE ** (-jnp.arange(HEAD_DIM // 2, dtype=f32) * 2.0 / HEAD_DIM)
 
     wide = 2 * HEAD_DIM
     key_width = KV_HEADS * HEAD_DIM
@@ -1099,58 +1525,47 @@
     )
     out_low = out_weight[0].astype(LOW)
     down_low = down_weight[0].astype(LOW)
-    gain_block = jnp.pad(norm_gains[0].astype(LOW), ((0, 14), (0, 128 - share)))
-    tok_all, cot_all, gain_all, mix_full, in_square, out_mine = first_exchange(
-        tokens, cotangent, gain_block, mix_blocks, in_blocks, out_low
+    rank = seq * 2 + fsdp
+    gain_block = lax.dynamic_update_slice(
+        jnp.zeros((16, 256), LOW), norm_gains[0].astype(LOW), (0, rank * share % 128)
+    )
+    (
+        mix_full,
+        out_mine,
+        in_mine,
+        down_mine,
+        gains,
+        normed_low,
+        query_t,
+        keys_r,
+        values_r,
+        pairs,
+        attended_t,
+        log_sum,
+        cosine,
+        sine,
+        middle,
+        two_all,
+    ) = forward(
+        lengths, frequency[:, None], tokens, gain_block, mix_blocks, out_low, in_blocks, down_low
     )
     rows = SQUARE * ROWS
-    tok_all = tok_all.reshape(rows, D)
-    cot_all = cot_all.reshape(rows, D)
-    gains = gain_all[:, :2, :share].transpose(1, 0, 2).reshape(2, D).astype(f32)
-    gain_attn, gain_mlp = gains[0], gains[1]
+    gain_attn, gain_mlp = gains[0, :D], gains[1, :D]
     mix_full = mix_full.reshape(D, 4 * HEAD_DIM)
     out_mine = out_mine.reshape(wide, D)
-    in_mine = four_parts(half, fsdp, in_square, 1).reshape(D, 8 * unit)
-    down_mine = four_parts(half, fsdp, down_low, 0).reshape(4 * unit, D)
-
-    normed_low = normalize(tok_all.astype(f32), gain_attn)[0].astype(LOW)
-    projected_t = dot32(mix_full, normed_low, ((0,), (1,)))
-    heads_t = turn(projected_t[: 3 * HEAD_DIM].reshape(3, HEAD_DIM, rows), cosine, sine).astype(LOW)
-    value_t = projected_t[3 * HEAD_DIM :].astype(LOW)
-    kinds = jnp.arange(6, dtype=jnp.int32)
-    query_t = jnp.concatenate(
-        [
-            heads_t[:2],
-            jnp.broadcast_to(
-                (segment[None, :] == kinds[:, None]).astype(LOW)[None], (2, 6, rows)
-            ),
-            jnp.zeros((2, 26, rows), LOW),
-        ],
-        axis=1,
-    )
-    key_value_t = jnp.concatenate([heads_t[2], value_t], axis=0)
-    arrived_t = lax.ppermute(key_value_t, "seq", [(i, i + SQUARE) for i in range(SQUARE)])
-    both_t = jnp.concatenate([arrived_t, key_value_t], axis=1)
-    keys_t, values_t = both_t[:HEAD_DIM], both_t[HEAD_DIM:]
-    all_segment = jnp.concatenate([other_segment, segment])
-    keys_r = jnp.concatenate(
-        [
-            keys_t.T,
-            jnp.where(all_segment[:, None] == kinds[None, :], 0.0, -WALL).astype(LOW),
-            jnp.zeros((2 * rows, 26), LOW),
-        ],
-        axis=1,
-    )
+    in_mine = in_mine.reshape(D, 8 * unit)
+    down_mine = down_mine.reshape(4 * unit, D)
+    normed_low = normed_low.reshape(rows, D)
+    two_all = two_all.reshape(rows, D)
+    stream = tokens.astype(f32)
+    cot_all = square_gather(cotangent)
+    attended_low = attended_t.astype(LOW)
+    places = half * KEYS + jnp.arange(KEYS, dtype=jnp.int32)
+    doc_lens = lax.dynamic_index_in_dim(lengths, fsdp, 0, keepdims=False)
+    keep_t = (places < jnp.sum(doc_lens)).astype(f32)[None, :]
     half_flag = half.astype(jnp.int32).reshape(1)
-    mixed_t, log_sum = attend(half_flag, query_t, keys_r, values_t)
-    attended_t = mixed_t.reshape(wide, rows) * keep_t
-    attended_low = attended_t.astype(LOW)
-    out_part = dot32(attended_low, out_mine, ((0,), (0,))).astype(LOW)
-    stream = tokens.astype(f32)
-    middle = stream + square_scatter(out_part)
-
-    normed_two, unit_mlp, scale_mlp = normalize(middle, gain_mlp)
-    two_all = square_gather(normed_two.astype(LOW))
+
+    _, unit_mlp, scale_mlp = normalize(middle, gain_mlp)
     gate_up = dot32(two_all, in_mine)
     gate, up = gate_up[:, : 4 * unit], gate_up[:, 4 * unit :]
     sigmoid_gate = jax.nn.sigmoid(gate)
@@ -1167,9 +1582,14 @@
     grad_stream = cotangent.astype(f32)
     grad_gain_mlp, grad_middle_norm = norm_backward(grad_normed_two, unit_mlp, scale_mlp, gain_mlp)
     grad_middle = grad_stream + grad_middle_norm
-    hidden_out = (middle + square_scatter(y_part)).astype(LOW)
-    in_sum = sum_half(sum_fsdp(grad_in.reshape(2, SQUARE, 2, share, 8 * unit), fsdp, 2), half)
-    down_sum = sum_half(sum_fsdp(grad_down.reshape(2, 2, unit, D), fsdp, 1), half)
+    grad_in = grad_in.reshape(2, SQUARE, 2, share, 8 * unit)
+    gate_x = sum_fsdp(grad_in[..., : 4 * unit], fsdp, 2)
+    grad_up_in, gate_x = lax.optimization_barrier((grad_in[..., 4 * unit :], gate_x))
+    up_x = sum_fsdp(grad_up_in, fsdp, 2)
+    gate_sum = sum_half(gate_x, half)
+    up_sum = sum_half(up_x, half)
+    grad_down, up_x = lax.optimization_barrier((grad_down, up_x))
+    down_x = sum_fsdp(grad_down.reshape(2, 2, unit, D), fsdp, 1)
 
     branch_all = square_gather(grad_middle.astype(LOW))
     grad_out = dot32(attended_low, branch_all)
@@ -1182,20 +1602,21 @@
     dq_t, dk, dv = attend_back(
         half_flag,
         query_t,
-        heads_t[:2].transpose(0, 2, 1),
+        query_t[:, :HEAD_DIM].transpose(0, 2, 1),
         keys_r,
-        keys_t,
-        values_t.T,
+        pairs[:, :HEAD_DIM].transpose(1, 0, 2).reshape(HEAD_DIM, 2 * KEYS),
+        values_r,
         grad_t,
         grad_t.transpose(0, 2, 1),
         log_sum,
         delta,
     )
     pair = jnp.concatenate([dk, dv], axis=1)
-    returned = lax.ppermute(
-        pair[:KEYS].astype(LOW), "seq", [(i + SQUARE, i) for i in range(SQUARE)]
-    )
-    pair_t = (pair[KEYS:] + returned.astype(f32)).T
+    returned, y_sum = return_exchange(pair[:KEYS].astype(LOW), y_part)
+    hidden_out = (middle + y_sum).astype(LOW)
+    down_x, returned = lax.optimization_barrier((down_x, returned))
+    down_sum = sum_half(down_x, half)
+    pair_t = (pair[KEYS:] + jnp.where(half == 0, returned.astype(f32), 0.0)).T
     scale = HEAD_DIM ** (-0.5)
     turned = turn(
         jnp.concatenate([dq_t, pair_t[None, :HEAD_DIM]], axis=0) * scale, cosine, -sine
@@ -1203,10 +1624,15 @@
     grad_projected_t = jnp.concatenate(
         [turned.reshape(3 * HEAD_DIM, rows), pair_t[HEAD_DIM:]], axis=0
     ).astype(LOW)
-    grad_mix = dot32(normed_low, grad_projected_t, ((0,), (1,)))
-    mix_sum = sum_half(sum_fsdp(grad_mix.reshape(2, SQUARE, 2, share, 4 * HEAD_DIM), fsdp, 2), half)
+    grad_mix = dot32(normed_low, grad_projected_t, ((0,), (1,))).astype(LOW)
     normed_part = dot32(grad_projected_t, mix_full, ((0,), (1,))).astype(LOW)
-    grad_normed = square_scatter(normed_part)
+    in_sum = jnp.concatenate([gate_sum.astype(LOW), up_sum.astype(LOW)], axis=-1)
+    grad_normed, mix_got, in_got, out_got = last_exchange(
+        normed_part,
+        grad_mix.reshape(SEQ, 2, share, 4 * HEAD_DIM),
+        in_sum,
+        out_sum.astype(LOW),
+    )
     _, unit_attn, scale_attn = normalize(stream, gain_attn)
     grad_gain_attn, grad_input_norm = norm_backward(grad_normed, unit_attn, scale_attn, gain_attn)
     grad_tokens = grad_middle + grad_input_norm
@@ -1214,9 +1640,6 @@
     gain_blocks = jnp.pad(
         jnp.stack([grad_gain_attn, grad_gain_mlp]).reshape(2, FLEET, share).transpose(1, 0, 2),
         ((0, 0), (0, 6), (0, 128 - share)),
-    )
-    in_got, mix_got, out_got, gain_got = last_exchange(
-        in_sum.astype(LOW), mix_sum.astype(LOW), out_sum.astype(LOW), gain_blocks
     )
     in_grad = (
         in_got.reshape(SQUARE, share, 2, 2, 2 * unit)
@@ -1232,15 +1655,14 @@
             mix_got[:, :, wide + HEAD_DIM :].reshape(share, key_width),
         ],
         axis=1,
-    ).astype(f32)[None]
+    )[None]
     out_grad = jnp.sum(out_got.astype(f32), axis=0)[None]
     down_grad = down_sum[None]
-    norm_grad = jnp.sum(gain_got[:, :2, :share], axis=0)[None]
-    squares = sum(
-        jnp.sum(grad * grad) for grad in (mix_grad, out_grad, in_grad, down_grad, norm_grad)
-    )
-    total_squares = jnp.sum(share_all(jnp.broadcast_to(squares, (8, 128)))[:, 0, 0])
-    grad_norm = jnp.sqrt(total_squares)
+    squares = sum(jnp.sum(grad * grad) for grad in (mix_grad, out_grad, in_grad, down_grad))
+    corner = jnp.zeros((8, 128), f32).at[0, 127].set(squares)
+    norm_got, totals = norm_exchange(gain_blocks, corner)
+    norm_grad = norm_got[None, :2, :share]
+    grad_norm = jnp.sqrt(jnp.sum(totals))
     clip_scale = CLIP_NORM / jnp.maximum(grad_norm, CLIP_NORM)
     results = [hidden_out, grad_tokens, grad_norm]
     for weight, first, second, grad, rate in (

time: 561 us -> 501 us (0.89)
  waiting for transfers between devices: 98.1 us -> 33.2 us
  Pallas kernels: 250 us -> 302 us
  other arithmetic: 76 us -> 42.9 us
  starting transfers between devices: 24.6 us -> 7.03 us
    pallas_call x4, Pallas kernels: 118 us -> 241 us  [the longest x1 130 us: forward(): pl.pallas_call(forward_kernel, out_shape=(shape((FLEET,) + mix.shape[1:],...]
    pallas_call x4 -> x1, Pallas kernels: 90 us -> 17.1 us  [square_scatter(): pl.pallas_call(scatter_kernel, out_shape=jax.ShapeDtypeStruct((ROWS, widt...]
    ppermute x2 -> x0, waiting for transfers between devices: 40.1 us -> none  [the longest x1 40.1 us: local_squares(): lax.ppermute(pair[:KEYS].astype(LOW), 'seq', [(i + SQUARE, i) for i in ra...]
    ppermute x5 -> x3, waiting for transfers between devices: 56.9 us -> 17.6 us  [swap_half(): return lax.ppermute(value, 'seq', [(i, i ^ SQUARE) for i in range(SEQ)])]
    ppermute x8 -> x4, waiting for transfers between devices: 1.12 us -> 15.6 us  [swap_fsdp(): return lax.ppermute(value, 'fsdp', [(0, 1), (1, 0)])]
    convert_element_type x11 -> x5, other arithmetic: 11.2 us -> 2.49 us  [the longest x1 0.8 us: local_squares(): norm_gains[0].astype(LOW)]
    select_n x6 -> x0, other arithmetic: 8.16 us -> none  [in_order(): jnp.where(flag == 0, jnp.stack([mine, other], axis=axis), jnp.stack([othe...]
    ppermute x2 -> x0, starting transfers between devices: 7.08 us -> none  [the longest x1 5.79 us: local_squares(): lax.ppermute(key_value_t, 'seq', [(i, i + SQUARE) for i in range(SQUARE)])]
  transfers between devices with their start and end apart: 15 -> 7, of which waited for: 4 -> 3; matrix products, arithmetic and copies ran while one was open for 16% -> 14% of each run, Pallas kernels for 36% -> 19%
where the time goes in v2:
time: 501 us; the launch traced here: 491 us
  Pallas kernels  302 us (60%)
  local copies, waits for them, and re-layouts  54.3 us (11%)
  matrix products  44.3 us (9%)
  other arithmetic  42.9 us (9%)
  waiting for transfers between devices  33.2 us (7%)
  between operations  7.32 us (1%)
  starting transfers between devices  7.03 us (1%)
    pallas_call x1, Pallas kernels, forward(): pl.pallas_call(forward_kernel, out_shape=(shape((FLEET,) + mix.shape[1:],...  130 us
    pallas_call x1, Pallas kernels, return_exchange(): pl.pallas_call(return_kernel, out_shape=(shape(pair.shape, LOW), shape((R...  52.9 us
    dot_general x10, matrix products, dot32(): lax.dot_general(left, right, (dims, ((), ())), preferred_element_type=jnp...  44.3 us
    pallas_call x1, Pallas kernels, last_exchange(): pl.pallas_call(last_kernel, out_shape=(shape((ROWS, width), jnp.float32),...  43.6 us
    pallas_call x2, Pallas kernels, square_gather(): pl.pallas_call(gather_kernel, out_shape=jax.ShapeDtypeStruct((SQUARE,) +...  37.4 us
    ppermute x3, waiting for transfers between devices, swap_half(): return lax.ppermute(value, 'seq', [(i, i ^ SQUARE) for i in range(SEQ)])  17.6 us
    pallas_call x1, Pallas kernels, square_scatter(): pl.pallas_call(scatter_kernel, out_shape=jax.ShapeDtypeStruct((ROWS, widt...  17.1 us
    ppermute x4, waiting for transfers between devices, swap_fsdp(): return lax.ppermute(value, 'fsdp', [(0, 1), (1, 0)])  15.6 us
  transfers between devices with their start and end apart: 7, of which 3 were waited for; matrix products, arithmetic and copies ran while one was open for 14% of the time, Pallas kernels for 19%

profile of v2, /device:TPU:0, one launch (start us, length us, event | category | flops | bytes accessed | tf_op | source)
XLA Modules:
  0.0 491.5 jit_solution(137933159899205318)
XLA Ops:
  1.3 1.2 convert_bitcast_fusion.1
  6.3 1.4 reshape.453.inn
  7.7 19.8 %square_gather.2 = bf16[8,128,1536]{2,1,0:T(8,128)(2,1)} custom-call(bf16[128,1536]{1,0:T(8,128)(2,1)} %src.1), custom_call_target="tpu_custom_call" | custom-call | tf_op jit(solution)/shard_map/square_gather/pallas_call | solution.py:617
  28.8 129.9 %forward.1 = (bf16[32,48,384]{2,1,0:T(8,128)(2,1)}, bf16[2,2,48,1536]{3,2,1,0:T(8,128)(2,1)}, bf16[2,8,2,48,1024]{4,3,2,1,0:T(8,128)(2,1)}, bf16[2,2,128,1536]{3...) custom-call(s32[2,5]{1,0:T(2,128)} %lengths.1, ...), custom_call_target="tpu_custom_call" | custom-call | tf_op jit(solution)/shard_map/forward/pallas_call | solution.py:1337
  158.6 4.8 copy.89
  163.5 5.6 %fusion.61 = f32[1024,1024]{0,1:T(8,128)S(1)} fusion(bf16[1024,1536]{1,0:T(8,128)(2,1)S(1)} %bitcast.188, bf16[1536,1024]{1,0:T(8,128)(2,1)} %bitcast.201), kind=kOutput, calls=%fused_computation.144 | convolution fusion | flops 3221225472 | bytes 10485760 | tf_op jit(solution)/shard_map/dot_general | solution.py:925
  169.1 3.5 fusion.5
  173.6 3.5 fusion
  177.2 2.4 fusion.57
  179.6 1.0 fusion.25
  180.6 1.5 collective-permute-start
  182.3 18.3 %convolution_convert_fusion.2 = bf16[1024,1536]{1,0:T(8,128)(2,1)S(1)} fusion(bf16[1536,1024]{1,0:T(8,128)(2,1)} %bitcast.202, bf16[1024,512]{0,1:T(8,128)(2,1)} %copy-done.72, bf16[1024,512]{0,1:T(8,128)(2,1)S(1)} %copy-done.71), kind=kOutput, calls=%fused_computation.2 | convolution fusion | flops 3226992640 | bytes 8388608 | tf_op jit(solution)/shard_map/dot_general | solution.py:925
  201.7 17.1 %square_scatter.1 = f32[128,1536]{1,0:T(8,128)S(1)} custom-call(bf16[8,128,1536]{2,1,0:T(8,128)(2,1)S(1)} %bitcast.176), custom_call_target="tpu_custom_call" | custom-call | tf_op jit(solution)/shard_map/square_scatter/pallas_call | solution.py:722
  219.8 1.0 fusion.46.src
  220.8 17.6 %square_gather.3 = bf16[8,128,1536]{2,1,0:T(8,128)(2,1)} custom-call(bf16[128,1536]{1,0:T(8,128)(2,1)} %fusion.46.src), custom_call_target="tpu_custom_call" | custom-call | tf_op jit(solution)/shard_map/square_gather/pallas_call | solution.py:617
  238.4 2.7 fusion.63
  241.2 1.0 copy-done.23
  242.2 1.3 collective-permute-start.5
  246.6 3.3 fusion.9
  250.2 1.2 multiply_reduce_fusion.3.delta
  251.5 1.0 copy-done.5
  252.5 1.0 copy-done.6
  253.5 6.5 %attend_back.1 = (f32[2,96,1024]{2,1,0:T(8,128)S(1)}, f32[2048,96]{1,0:T(8,128)S(1)}, f32[2048,96]{1,0:T(8,128)}) custom-call(s32[1]{0:T(128)} %bitcast.6.half, bf16[2,128,1024]{2,1,0:T(8,128)(2,1)S(1)} %copy-done, bf16[2,1024,96]{2,1,0:T(8,128)(2,1)S(1)} %slice_bitcast_fusion.1.queries_r, bf16[2048,128]{1,0:T(8,128)(2,1)S(1)} %copy-done.5, ...), custom_call_target="tpu_custom_call" | custom-call | tf_op jit(solution)/shard_map/attend_back/pallas_call | solution.py:1422
  260.1 1.6 fusion.11.pair
  262.2 1.8 convolution_convert_fusion.1
  264.1 52.9 %return_exchange.1 = (bf16[1024,192]{1,0:T(8,128)(2,1)S(1)}, f32[128,1536]{1,0:T(8,128)S(1)}) custom-call(bf16[1024,192]{1,0:T(8,128)(2,1)S(1)} %fusion.11.pair, bf16[8,128,1536]{2,1,0:T(8,128)(2,1)S(1)} %bitcast.174), custom_call_target="tpu_custom_call" | custom-call | tf_op jit(solution)/shard_map/return_exchange/pallas_call | solution.py:752
  317.0 1.7 bitcast_add_fusion.2
  321.6 1.8 fusion.62
  323.5 15.6 %collective-permute-done.1 = bf16[2,8,48,512]{3,2,1,0:T(8,128)(2,1)S(1)} collective-permute-done((bf16[2,8,48,512]{3,2,1,0:T(8,128)(2,1)S(1)}, bf16[2,8,48,512]{3,2,1,0:T(8,128)(2,1)S(1)}, u32[]{:S(2)}, u32[]{:S(2)}) %collective-permute-start.1) | collective-permute-done | bytes 786464 | tf_op jit(solution)/shard_map/ppermute | solution.py:1437
  340.7 1.0 fusion.31.out
  341.7 9.4 %collective-permute-done.3 = bf16[8,48,512]{2,1,0:T(8,128)(2,1)S(1)} collective-permute-done((bf16[8,48,512]{2,1,0:T(8,128)(2,1)S(1)}, bf16[8,48,512]{2,1,0:T(8,128)(2,1)S(1)}, u32[]{:S(2)}, u32[]{:S(2)}) %collective-permute-start.3) | collective-permute-done | bytes 393248 | tf_op jit(solution)/shard_map/ppermute | solution.py:1441
  351.2 8.2 %collective-permute-done.4 = bf16[8,48,512]{2,1,0:T(8,128)(2,1)S(1)} collective-permute-done((bf16[8,48,512]{2,1,0:T(8,128)(2,1)S(1)}, bf16[8,48,512]{2,1,0:T(8,128)(2,1)S(1)}, u32[]{:S(2)}, u32[]{:S(2)}) %collective-permute-start.4) | collective-permute-done | bytes 393248 | tf_op jit(solution)/shard_map/ppermute | solution.py:1441
  359.7 1.3 bitcast_add_fusion
  363.4 1.1 maximum_multiply_fusion
  365.5 1.1 copy-done.64
  366.6 1.8 convolution_convert_fusion.3
  368.5 1.8 convolution_convert_fusion
  370.3 43.6 %last_exchange.1 = (f32[128,1536]{1,0:T(8,128)S(1)}, f32[8,48,384]{2,1,0:T(8,128)S(1)}, bf16[8,48,1024]{2,1,0:T(8,128)(2,1)S(1)}, bf16[2,48,1536]{2,1,0:T(8,128)(2,1)S(1)}) custom-call(bf16[8,128,1536]{2,1,0:T(8,128)(2,1)S(1)} %bitcast.175, bf16[16,2,48,384]{3,2,1,0:T(8,128)(2,1)S(1)} %bitcast.179, bf16[8,48,1024]{2,1,0:T(8,128)(2,1)S(1)} %pad_maximum_fusion.5.inn, ...), custom_call_target="tpu_custom_call" | custom-call | tf_op jit(solution)/shard_map/last_exchange/pallas_call | solution.py:858
  414.8 1.9 fusion.34
  416.7 2.4 collective-permute-start.6
  419.2 1.0 multiply_reduce_fusion
  421.7 1.0 convert_reduce_fusion
  426.0 1.7 copy.98
  427.7 1.7 concatenate.64
  429.4 1.8 concatenate.63
  431.3 1.1 constant_dynamic-update-slice_fusion.2
  435.9 1.4 fusion.20
  437.3 1.7 reshape.477
  439.0 1.7 reshape.476
  440.7 1.8 reshape.475
  442.6 1.5 reshape.479
  444.1 2.1 copy.103
  446.2 1.7 reshape.478
  450.6 2.0 maximum_bitcast_fusion
  452.6 2.6 fusion.45
  456.6 1.4 scatter.4.squares
  458.6 15.1 %norm_exchange.1 = (f32[8,128]{1,0:T(8,128)}, f32[8,128]{1,0:T(8,128)}) custom-call(f32[32,8,128]{2,1,0:T(8,128)} %pad.8.gain, f32[8,128]{1,0:T(8,128)} %copy-done.52), custom_call_target="tpu_custom_call" | custom-call | tf_op jit(solution)/shard_map/norm_exchange/pallas_call | solution.py:910
  473.7 1.3 reduce_sum.139
  475.7 1.4 slice_bitcast_fusion.3
  477.1 1.3 fusion.47
  478.4 2.4 fusion.53
  480.8 2.9 fusion.55
  483.7 3.3 fusion.51
  487.0 3.0 fusion.49
  (218 shorter events, 31.3 us)
Async XLA Ops:
  0.7 2.7 copy-start.40
  1.3 3.3 copy-start.32
  2.5 2.9 copy-start.17
  158.6 4.8 copy-start.29
  163.5 5.6 %copy-start.27 = (bf16[8,128,1536]{2,1,0:T(8,128)(2,1)S(1)}, bf16[8,128,1536]{2,1,0:T(8,128)(2,1)}, u32[]{:S(2)}) copy-start(bf16[8,128,1536]{2,1,0:T(8,128)(2,1)} %square_gather.2) | copy-start | bytes 9437188
  163.5 5.7 %copy-start.65 = (bf16[2,2,128,1536]{3,2,1,0:T(8,128)(2,1)S(1)}, bf16[2,2,128,1536]{3,2,1,0:T(8,128)(2,1)}, u32[]{:S(2)}) copy-start(bf16[2,2,128,1536]{3,2,1,0:T(8,128)(2,1)} %get-tuple-element.78) | copy-start | bytes 4718596
  169.1 4.5 copy-start.30
  172.7 4.5 copy-start.72
  179.6 20.9 %copy-start.12 = (f32[2,8,2,48,512]{4,3,1,0,2:T(8,128)}, f32[2,8,2,48,512]{4,3,1,0,2:T(8,128)S(1)}, u32[]{:S(2)}) copy-start(f32[2,8,2,48,512]{4,3,1,0,2:T(8,128)S(1)} %get-tuple-element.130) | copy-start | bytes 9437188
  179.6 2.5 copy-start.15
  179.6 2.6 copy-start.71
  180.6 136.3 %collective-permute-start = (bf16[2,8,48,512]{3,2,1,0:T(8,128)(2,1)}, bf16[2,8,48,512]{3,2,1,0:T(8,128)(2,1)}, u32[]{:S(2)}, u32[]{:S(2)}) collective-permute-start(bf16[2,8,48,512]{3,2,1,0:T(8,128)(2,1)} %fusion.25), channel_id=1, source_target_pairs={{0,1},{1,0},{2,3},{3,2},{4,5},{5,4},{6,7},{7,6},{8,9},{9,8},{10,11... | collective-permute-start | bytes 2359304 | tf_op jit(solution)/shard_map/ppermute | solution.py:1437
  182.3 18.3 %copy-start.9 = (f32[128,1536]{1,0:T(8,128)S(1)}, f32[128,1536]{1,0:T(8,128)}, u32[]{:S(2)}) copy-start(f32[128,1536]{1,0:T(8,128)} %get-tuple-element.72) | copy-start | bytes 2359300
  182.3 19.4 %copy-start.31 = (f32[192,1024]{1,0:T(8,128)S(1)}, f32[192,1024]{1,0:T(8,128)}, u32[]{:S(2)}) copy-start(f32[192,1024]{1,0:T(8,128)} %get-tuple-element.83) | copy-start | bytes 2359300
  218.8 2.0 copy-start.53
  218.8 201.4 %copy-start.55 = (f32[128]{0:T(128)}, f32[128]{0:T(128)S(1)}, u32[]{:S(2)}) copy-start(f32[128]{0:T(128)S(1)} %get-tuple-element.147) | copy-start | bytes 1540
  219.8 18.6 %copy-start.57 = (f32[128]{0:T(128)}, f32[128]{0:T(128)S(1)}, u32[]{:S(2)}) copy-start(f32[128]{0:T(128)S(1)} %broadcast_multiply_fusion.1) | copy-start | bytes 1540
  238.4 5.2 %copy-start.59 = (s32[2,5]{1,0:T(2,128)S(1)}, s32[2,5]{1,0:T(2,128)}, u32[]{:S(2)}) copy-start(s32[2,5]{1,0:T(2,128)} %lengths.1) | copy-start | bytes 124
  238.4 5.8 %copy-start.48 = (f32[48,1024]{1,0:T(8,128)S(1)}, f32[48,1024]{1,0:T(8,128)}, u32[]{:S(2)}) copy-start(f32[48,1024]{1,0:T(8,128)} %get-tuple-element.93) | copy-start | bytes 589828
  238.4 6.5 %copy-start.47 = (bf16[8,192,256]{2,1,0:T(8,128)(2,1)S(1)}, bf16[8,192,256]{2,1,0:T(8,128)(2,1)}, u32[]{:S(2)}) copy-start(bf16[8,192,256]{2,1,0:T(8,128)(2,1)} %get-tuple-element.75) | copy-start | bytes 2359300
  242.2 2.8 copy-start
  242.2 98.3 %collective-permute-start.5 = (bf16[2,48,1536]{2,1,0:T(8,128)(2,1)S(1)}, bf16[2,48,1536]{2,1,0:T(8,128)(2,1)}, u32[]{:S(2)}, u32[]{:S(2)}) collective-permute-start(bf16[2,48,1536]{2,1,0:T(8,128)(2,1)S(1)} %fusion.36), channel_id=1, source_target_pairs={{0,1},{1,0},{2,3},{3,2},{4,5},{5,4},{6,7},{7,6},{8,9},{9,8},{10,11... | collective-permute-start | bytes 884744 | tf_op jit(solution)/shard_map/ppermute | solution.py:1437
  260.1 4.0 copy-start.3
  260.1 1.8 copy-start.66
  260.1 2.1 copy-start.69
  262.2 59.4 %copy-start.28 = (bf16[8,128,1536]{2,1,0:T(8,128)(2,1)S(1)}, bf16[8,128,1536]{2,1,0:T(8,128)(2,1)}, u32[]{:S(2)}) copy-start(bf16[8,128,1536]{2,1,0:T(8,128)(2,1)} %square_gather.2) | copy-start | bytes 9437188
  264.0 52.9 %copy-start.13 = (f32[2,8,2,48,512]{4,3,1,0,2:T(8,128)S(1)}, f32[2,8,2,48,512]{4,3,1,0,2:T(8,128)}, u32[]{:S(2)}) copy-start(f32[2,8,2,48,512]{4,3,1,0,2:T(8,128)} %copy-done.12) | copy-start | bytes 9437188
  316.9 1.8 copy-start.1
  317.0 2.4 copy-start.11
  318.7 2.2 copy-start.68
  319.5 19.6 %collective-permute-start.1 = (bf16[2,8,48,512]{3,2,1,0:T(8,128)(2,1)S(1)}, bf16[2,8,48,512]{3,2,1,0:T(8,128)(2,1)S(1)}, u32[]{:S(2)}, u32[]{:S(2)}) collective-permute-start(bf16[2,8,48,512]{3,2,1,0:T(8,128)(2,1)S(1)} %fusion.26), channel_id=1, source_target_pairs={{0,1},{1,0},{2,3},{3,2},{4,5},{5,4},{6,7},{7,6},{8,9},{9,8},{10,11... | collective-permute-start | bytes 2359304 | tf_op jit(solution)/shard_map/ppermute | solution.py:1437
  323.4 27.7 %collective-permute-start.3 = (bf16[8,48,512]{2,1,0:T(8,128)(2,1)S(1)}, bf16[8,48,512]{2,1,0:T(8,128)(2,1)S(1)}, u32[]{:S(2)}, u32[]{:S(2)}) collective-permute-start(bf16[8,48,512]{2,1,0:T(8,128)(2,1)S(1)} %fusion.32), channel_id=1, source_target_pairs={{0,16},{2,18},{4,20},{6,22},{8,24},{10,26},{12,28},{14,30},{16,0},... | collective-permute-start | bytes 1179656 | tf_op jit(solution)/shard_map/ppermute | solution.py:1441
  339.5 19.9 %collective-permute-start.4 = (bf16[8,48,512]{2,1,0:T(8,128)(2,1)S(1)}, bf16[8,48,512]{2,1,0:T(8,128)(2,1)S(1)}, u32[]{:S(2)}, u32[]{:S(2)}) collective-permute-start(bf16[8,48,512]{2,1,0:T(8,128)(2,1)S(1)} %fusion.33), channel_id=1, source_target_pairs={{0,16},{2,18},{4,20},{6,22},{8,24},{10,26},{12,28},{14,30},{16,0},... | collective-permute-start | bytes 1179656 | tf_op jit(solution)/shard_map/ppermute | solution.py:1441
  339.7 20.0 %collective-permute-start.2 = (bf16[2,128,1536]{2,1,0:T(8,128)(2,1)S(1)}, bf16[2,128,1536]{2,1,0:T(8,128)(2,1)S(1)}, u32[]{:S(2)}, u32[]{:S(2)}) collective-permute-start(bf16[2,128,1536]{2,1,0:T(8,128)(2,1)S(1)} %fusion.27), channel_id=1, source_target_pairs={{0,1},{1,0},{2,3},{3,2},{4,5},{5,4},{6,7},{7,6},{8,9},{9,8},{10,11... | collective-permute-start | bytes 2359304 | tf_op jit(solution)/shard_map/ppermute | solution.py:1437
  361.5 2.0 copy-start.4
  362.6 2.0 copy-start.41
  362.6 2.0 copy-start.45
  364.6 2.0 copy-start.64
  366.6 1.9 copy-start.67
  413.9 6.2 %copy-start.7 = (bf16[2,48,1536]{2,1,0:T(8,128)(2,1)}, bf16[2,48,1536]{2,1,0:T(8,128)(2,1)S(1)}, u32[]{:S(2)}) copy-start(bf16[2,48,1536]{2,1,0:T(8,128)(2,1)S(1)} %get-tuple-element.99) | copy-start | bytes 884740
  414.0 6.2 %copy-start.16 = (bf16[128,1536]{1,0:T(8,128)(2,1)S(1)}, bf16[128,1536]{1,0:T(8,128)(2,1)}, u32[]{:S(2)}) copy-start(bf16[128,1536]{1,0:T(8,128)(2,1)} %tok.1) | copy-start | bytes 1179652
  416.7 35.9 %collective-permute-start.6 = (bf16[128,1536]{1,0:T(8,128)(2,1)}, bf16[128,1536]{1,0:T(8,128)(2,1)}, u32[]{:S(2)}, u32[]{:S(2)}) collective-permute-start(bf16[128,1536]{1,0:T(8,128)(2,1)} %fusion.34), channel_id=1, source_target_pairs={{0,16},{2,18},{4,20},{6,22},{8,24},{10,26},{12,28},{14,30},{16,0},... | collective-permute-start | bytes 1179656 | tf_op jit(solution)/shard_map/ppermute | solution.py:1441
  426.0 9.8 %copy-start.2 = (f32[128,1536]{1,0:T(8,128)S(1)}, f32[128,1536]{1,0:T(8,128)}, u32[]{:S(2)}) copy-start(f32[128,1536]{1,0:T(8,128)} %copy-done.1) | copy-start | bytes 2359300
  431.3 4.5 copy-start.10
  431.3 4.5 copy-start.26
  431.3 4.5 copy-start.54
  431.3 4.5 copy-start.56
  431.3 4.5 copy-start.58
  431.3 4.5 copy-start.63
  446.2 6.4 %copy-start.14 = (f32[2,128,1536]{2,1,0:T(8,128)S(1)}, f32[2,128,1536]{2,1,0:T(8,128)}, u32[]{:S(2)}) copy-start(f32[2,128,1536]{2,1,0:T(8,128)} %bitcast_add_fusion) | copy-start | bytes 4718596
  447.9 35.8 %copy-start.19 = (f32[1,48,8192]{2,1,0:T(8,128)}, f32[1,48,8192]{2,1,0:T(8,128)S(1)}, u32[]{:S(2)}) copy-start(f32[1,48,8192]{2,1,0:T(8,128)S(1)} %reshape.478) | copy-start | bytes 4718596
  450.6 26.5 %copy-start.60 = (f32[1,2,48]{2,1,0:T(2,128)S(1)}, f32[1,2,48]{2,1,0:T(2,128)}, u32[]{:S(2)}) copy-start(f32[1,2,48]{2,1,0:T(2,128)} %param.27) | copy-start | bytes 1156
  450.6 26.5 %copy-start.61 = (f32[1,2,48]{2,1,0:T(2,128)S(1)}, f32[1,2,48]{2,1,0:T(2,128)}, u32[]{:S(2)}) copy-start(f32[1,2,48]{2,1,0:T(2,128)} %param.32) | copy-start | bytes 1156
  450.6 26.5 %copy-start.62 = (f32[1,2,48]{2,1,0:T(2,128)S(1)}, f32[1,2,48]{2,1,0:T(2,128)}, u32[]{:S(2)}) copy-start(f32[1,2,48]{2,1,0:T(2,128)} %param.37) | copy-start | bytes 1156
  450.6 27.8 %copy-start.35 = (f32[48,1536]{1,0:T(8,128)S(1)}, f32[48,1536]{1,0:T(8,128)}, u32[]{:S(2)}) copy-start(f32[48,1536]{1,0:T(8,128)} %copy-done.34) | copy-start | bytes 884740
  475.7 5.1 %copy-start.22 = (f32[1,48,3072]{2,1,0:T(8,128)S(1)}, f32[1,48,3072]{2,1,0:T(8,128)}, u32[]{:S(2)}) copy-start(f32[1,48,3072]{2,1,0:T(8,128)} %copy-done.21) | copy-start | bytes 1769476
  475.7 5.1 %copy-start.36 = (f32[1,48,3072]{2,1,0:T(8,128)S(1)}, f32[1,48,3072]{2,1,0:T(8,128)}, u32[]{:S(2)}) copy-start(f32[1,48,3072]{2,1,0:T(8,128)} %param.23) | copy-start | bytes 1769476
  475.7 5.0 %copy-start.44 = (f32[1,48,3072]{2,1,0:T(8,128)S(1)}, f32[1,48,3072]{2,1,0:T(8,128)}, u32[]{:S(2)}) copy-start(f32[1,48,3072]{2,1,0:T(8,128)} %param.28) | copy-start | bytes 1769476
  478.4 5.3 %copy-start.39 = (f32[1,48,8192]{2,1,0:T(8,128)S(1)}, f32[1,48,8192]{2,1,0:T(8,128)}, u32[]{:S(2)}) copy-start(f32[1,48,8192]{2,1,0:T(8,128)} %param.35) | copy-start | bytes 4718596
  480.8 2.9 copy-start.18
  480.8 2.9 copy-start.38
  483.7 3.3 copy-start.33
  483.7 3.3 copy-start.42
  483.7 3.3 copy-start.43
  (16 other events, 17.0 us)
